TPU v7x, 512 devices: a whole 4x8x8 slice. The times are simulated.
512 devices in a mesh: dp: 64 (over y_hi, z, core), tensor: 8 (over y_lo, x).
Axes of the slice: x: 4, y: 8 (y_hi: 4, y_lo: 2; y = y_hi * 2 + y_lo), z: 8, core: 2. Of those that a mesh axis runs over, the one named last changes fastest.
Arguments:
- q_base: bfloat16 [16384, 8192], P('dp', 'tensor'), may hold values from -48 to 48
- kv_base: bfloat16 [2, 16384, 1024], P(None, 'dp', 'tensor'), may hold values from -6 to 6
- cotangent: bfloat16 [16384, 8192], P('dp', 'tensor'), may hold values from -6 to 6
- steering: float32 [8192], P('dp'), may hold values from -6 to 6
- w_query: bfloat16 [8192, 8192], P('dp', 'tensor'), may hold values from -0.0625 to 0.0625
- w_kv: bfloat16 [2, 8192, 1024], P(None, 'dp', 'tensor'), may hold values from -0.0625 to 0.0625
- prompt_cache: bfloat16 [2, 32, 1024, 1024], P(None, None, 'dp', 'tensor'), may hold values from -6 to 6
- prompt_ids: int32 [64], P('dp'), may hold values from 0 to 31
- dialogue_lens: int32 [64], P('dp'), may hold values from 64 to 256, as said below
- prompt_lens: int32 [32], replicated, may hold values from 256 to 1024, as said below
Outputs:
- query_grad: bfloat16 [16384, 8192], P('dp', 'tensor')
- kv_grad: bfloat16 [2, 16384, 1024], P(None, 'dp', 'tensor')
- steer_grad: float32 [8192], P('dp')
Inputs may be any that keep to these rules, and one draw needn't show every extreme that they name: `dialogue_lens`: some dialogue has all 256 tokens live. `prompt_lens`: some prompt has all 1024 positions live.
All inputs are finite; a program needn't handle non-finite values.
Results may differ from a plain program's by a relative error of at most 0.0121.
Values may be sent and summed in bfloat16 or wider, within the bound.
No kernel may reach another device: no remote copies, remote signals or barrier semaphores. Data moves between devices by JAX's collectives and lax.ppermute only.
A program may use at most 64 MiB of HBM per device.

v0:
```python
import math

import jax
import jax.numpy as jnp
from jax import lax
from jax.sharding import PartitionSpec as P

HD = 128


def scores_of(queries, pre_keys, own_keys, pre_mask, own_mask, score_scale):
    pre_scores = (
        jnp.einsum("tgd,pd->tgp", queries, pre_keys, preferred_element_type=jnp.float32)
        * score_scale
    )
    own_scores = (
        jnp.einsum("tgd,ud->tgu", queries, own_keys, preferred_element_type=jnp.float32)
        * score_scale
    )
    pre_scores = jnp.where(pre_mask[None, None, :], pre_scores, -jnp.inf)
    own_scores = jnp.where(own_mask[:, None, :], own_scores, -jnp.inf)
    return (pre_scores, own_scores)


def statistics(pre_scores, own_scores):
    maxima = jnp.maximum(jnp.max(pre_scores, -1), jnp.max(own_scores, -1))
    totals = jnp.sum(jnp.exp(pre_scores - maxima[..., None]), -1) + jnp.sum(
        jnp.exp(own_scores - maxima[..., None]), -1
    )
    return (maxima, totals)


def backward_of(
    queries,
    pre_keys,
    pre_values,
    own_keys,
    own_values,
    grad_out,
    pre_scores,
    own_scores,
    maxima,
    totals,
    score_scale,
):
    pre_probs = jnp.exp(pre_scores - maxima[..., None]) / totals[..., None]
    own_probs = jnp.exp(own_scores - maxima[..., None]) / totals[..., None]
    pre_weights = pre_probs.astype(jnp.bfloat16)
    own_weights = own_probs.astype(jnp.bfloat16)
    attended = jnp.einsum(
        "tgp,pd->tgd", pre_weights, pre_values, preferred_element_type=jnp.float32
    ) + jnp.einsum("tgu,ud->tgd", own_weights, own_values, preferred_element_type=jnp.float32)
    delta = jnp.sum(grad_out.astype(jnp.float32) * attended, -1)
    pre_gw = jnp.einsum("tgd,pd->tgp", grad_out, pre_values, preferred_element_type=jnp.float32)
    own_gw = jnp.einsum("tgd,ud->tgu", grad_out, own_values, preferred_element_type=jnp.float32)
    pre_gs = (pre_probs * (pre_gw - delta[..., None]) * score_scale).astype(jnp.bfloat16)
    own_gs = (own_probs * (own_gw - delta[..., None]) * score_scale).astype(jnp.bfloat16)
    grad_query = jnp.einsum(
        "tgp,pd->tgd", pre_gs, pre_keys, preferred_element_type=jnp.float32
    ) + jnp.einsum("tgu,ud->tgd", own_gs, own_keys, preferred_element_type=jnp.float32)
    grad_key = jnp.einsum("tgu,tgd->ud", own_gs, queries, preferred_element_type=jnp.float32)
    grad_value = jnp.einsum(
        "tgu,tgd->ud", own_weights, grad_out, preferred_element_type=jnp.float32
    )
    return (grad_query, grad_key, grad_value)


def shards(
    q_base,
    kv_base,
    cotangent,
    steering,
    w_query,
    w_kv,
    prompt_cache,
    prompt_ids,
    dialogue_lens,
    prompt_lens,
):
    precise = lax.Precision.HIGHEST
    part_q = jnp.dot(steering, w_query.astype(jnp.float32), precision=precise)
    part_kv = jnp.einsum("d,cdk->ck", steering, w_kv.astype(jnp.float32), precision=precise)
    shift_q, shift_kv = lax.psum((part_q, part_kv), "dp")
    query = (q_base.astype(jnp.float32) + shift_q[None, :]).astype(jnp.bfloat16)
    keys_values = (kv_base.astype(jnp.float32) + shift_kv[:, None, :]).astype(jnp.bfloat16)
    dp_count = lax.axis_size("dp")
    dial_count = prompt_ids.shape[0]
    all_ids = lax.all_gather(prompt_ids, "dp", axis=0, tiled=True)
    id_table = all_ids.reshape(dp_count, dial_count).T
    pos_block = prompt_cache.shape[2]
    kv_width = prompt_cache.shape[3]
    prompt_span = dp_count * pos_block
    heads_kv = kv_width // HD
    heads_q = query.shape[1] // HD
    group_size = heads_q // heads_kv
    dial_len = query.shape[0] // dial_count
    score_scale = 1.0 / math.sqrt(HD)
    id_match = prompt_ids[:, None] == jnp.arange(prompt_lens.shape[0], dtype=jnp.int32)[None, :]
    own_prompt_lens = jnp.sum(jnp.where(id_match, prompt_lens[None, :], 0), axis=1)
    places = jnp.arange(dial_len, dtype=jnp.int32)
    prompt_places = jnp.arange(prompt_span, dtype=jnp.int32)

    def by_head(rows):
        return rows.reshape(prompt_span, heads_kv, HD).transpose(1, 0, 2)

    grad_queries = []
    grad_keys = []
    grad_values = []

    def collect(outputs):
        grad_query, grad_key, grad_value = outputs
        grad_queries.append(grad_query.transpose(1, 0, 2, 3).reshape(dial_len, heads_q * HD))
        grad_keys.append(grad_key.transpose(1, 0, 2).reshape(dial_len, kv_width))
        grad_values.append(grad_value.transpose(1, 0, 2).reshape(dial_len, kv_width))

    outgoing = prompt_cache[:, id_table]
    arrived = lax.all_to_all(outgoing, "dp", split_axis=2, concat_axis=2, tiled=True).reshape(
        2, dial_count, prompt_span, kv_width
    )
    queries = query.reshape(dial_len, heads_kv, group_size, HD).transpose(1, 0, 2, 3)
    own_kv = keys_values.reshape(2, dial_len, heads_kv, HD).transpose(0, 2, 1, 3)
    live = dialogue_lens[0]
    grads = cotangent
    grads = jnp.where((places < live)[:, None], grads, jnp.zeros_like(grads))
    grads = grads.reshape(dial_len, heads_kv, group_size, HD).transpose(1, 0, 2, 3)
    prepare_own_mask = (places[None, :] <= places[:, None]) & (places[None, :] < live)
    prepare_pre_mask = prompt_places < own_prompt_lens[0]
    queries, own_kv, grads, own_mask, pre_mask = (
        queries,
        own_kv,
        grads,
        prepare_own_mask,
        prepare_pre_mask,
    )
    pre_keys = by_head(arrived[0, 0])
    pre_values = by_head(arrived[1, 0])

    def whole_head(inputs):
        q_head, pk_head, pv_head, ok_head, ov_head, g_head = inputs
        pre_scores, own_scores = scores_of(
            q_head, pk_head, ok_head, pre_mask, own_mask, score_scale
        )
        maxima, totals = statistics(pre_scores, own_scores)
        return backward_of(
            q_head,
            pk_head,
            pv_head,
            ok_head,
            ov_head,
            g_head,
            pre_scores,
            own_scores,
            maxima,
            totals,
            score_scale,
        )

    collect(lax.map(whole_head, (queries, pre_keys, pre_values, own_kv[0], own_kv[1], grads)))
    query_full = grad_queries[0]
    kv_full = jnp.stack([grad_keys[0], grad_values[0]])
    total_q, total_kv = lax.psum((jnp.sum(query_full, 0), jnp.sum(kv_full, 1)), "dp")
    steer_part = jnp.dot(w_query.astype(jnp.float32), total_q, precision=precise) + jnp.einsum(
        "cdk,ck->d", w_kv.astype(jnp.float32), total_kv, precision=precise
    )
    steer_grad = lax.psum(steer_part, "tensor")
    return (query_full.astype(jnp.bfloat16), kv_full.astype(jnp.bfloat16), steer_grad)


def solution(mesh):
    placed = (
        P("dp", "tensor"),
        P(None, "dp", "tensor"),
        P("dp", "tensor"),
        P("dp"),
        P("dp", "tensor"),
        P(None, "dp", "tensor"),
        P(None, None, "dp", "tensor"),
        P("dp"),
        P("dp"),
        P(),
    )
    return jax.shard_map(
        shards,
        mesh=mesh,
        in_specs=placed,
        out_specs=(P("dp", "tensor"), P(None, "dp", "tensor"), P("dp")),
        check_vma=False,
    )
```

profile of v0, /device:TPU:1, one launch (start us, length us, event | category | flops | bytes accessed | tf_op | source)
XLA Modules:
  0.0 373.3 jit_solution(17652566416198620623)
XLA Ops:
  0.6 0.0 copy-start
  1.4 1.3 dynamic-slice
  2.7 0.8 dynamic-update-slice
  3.4 26.3 %all-reduce = s32[64]{0:T(128)S(1)} all-reduce(s32[64]{0:T(128)S(1)} %dynamic-update-slice), channel_id=1, replica_groups=mesh['dp'=64,'tensor'=8] {'dp'}, use_global_device_ids=true, to_apply=%add | all-reduce | flops 64 | bytes 512
  29.8 1.5 gather_fusion
  31.3 8.9 %all-to-all-start = ((bf16[2,1,64,16,128]{4,3,0,1,2:T(8,128)(2,1)}), bf16[2,1,64,16,128]{4,3,0,1,2:T(8,128)(2,1)S(1)}, u32[]{:S(2)}, u32[]{:S(2)}) async-start(bf16[2,1,64,16,128]{4,3,0,1,2:T(8,128)(2,1)} %bitcast.7), calls=%async_computation | async-start | bytes 1048576 | tf_op jit(solution)/shard_map/all_to_all | solution.py:117
  40.9 0.2 fusion.35
  41.1 0.1 broadcast_select_fusion
  41.2 0.1 fusion.33
  41.3 1.1 copy.59
  42.4 144.1 %all-reduce.2 = (f32[1024]{0:T(1024)S(1)}, f32[2,128]{1,0:T(2,128)S(1)}) all-reduce(f32[1024]{0:T(1024)S(1)} %bitcast.111, f32[2,128]{1,0:T(2,128)S(1)} %bitcast.113), channel_id=1, replica_groups=mesh['dp'=64,'tensor'=8] {'dp'}, use_global_device_ids=true, to_apply=%region_1.0 | all-reduce | flops 1280 | bytes 10240 | tf_op jit(solution)/shard_map/psum | solution.py:83
  186.6 0.6 fusion.32
  187.2 0.6 iota_compare_fusion.1
  187.9 0.1 fusion.29
  188.0 0.7 add_convert_fusion.1
  188.7 1.3 fusion.10
  190.1 1.4 fusion
  191.5 0.4 fusion.12
  192.0 2.2 fusion.2
  194.3 0.6 convolution_bitcast_fusion
  194.9 2.5 fusion.5
  197.5 2.2 fusion.16
  199.6 7.5 %fusion.3 = f32[256,8,128]{0,2,1:T(8,128)S(1)} fusion(bf16[1024,128,1]{1,0,2:T(8,128)(2,1)} %bitcast.103, f32[256,8]{0,1:T(8,128)} %fusion.16, bf16[256,8,128]{0,2,1:T(8,128)(2,1)} %bitcast.104, bf16[1024,128,1]{1,0,2:T(8,128)(2,1)} %bitcast.109, f32[256,8,1024]{2,0,1:T(8,128)} %copy-done.1, f32[256,8]{0,1:T(8,128)S(1)} %add.60, f32[256,8]{0,1:T(8,128)S(1)} %max.8, ...), kind=kOutput, calls=%fused_computation.7 | convolution fusion | flops 1090519040 | bytes 10511360 | tf_op jit(solution)/shard_map/while/body/eval_jaxpr/tgp,pd->tgd/dot_general | solution.py:58
  207.2 1.9 multiply_convert_fusion.2
  209.1 0.4 convolution_bitcast_fusion.1
  209.6 0.7 fusion.31
  210.3 1.4 fusion.43
  211.6 1.0 copy.72
  212.6 143.1 %all-reduce.1 = (f32[1024]{0:T(1024)S(1)}, f32[2,128]{1,0:T(2,128)S(1)}) all-reduce(f32[1024]{0:T(1024)S(1)} %bitcast.110, f32[2,128]{1,0:T(2,128)S(1)} %fusion.30), channel_id=1, replica_groups=mesh['dp'=64,'tensor'=8] {'dp'}, use_global_device_ids=true, to_apply=%region_9.10 | all-reduce | flops 1280 | bytes 10240 | tf_op jit(solution)/shard_map/psum | solution.py:161
  355.8 0.3 convolution_bitcast_fusion.3
  356.1 0.1 fusion.17
  356.2 17.0 %psum.39 = f32[128]{0:T(128)} all-reduce(f32[128]{0:T(128)S(1)} %fusion.17), channel_id=1, replica_groups=mesh['dp'=64,'tensor'=8] {'tensor'}, use_global_device_ids=true, to_apply=%region_12.13 | all-reduce | flops 128 | bytes 1024 | tf_op jit(solution)/shard_map/psum | solution.py:165
  (50 shorter events, 0.2 us)
Async XLA Ops:
  0.6 29.1 %copy-start = (bf16[2,32,16,128]{3,2,1,0:T(8,128)(2,1)S(1)}, bf16[2,32,16,128]{3,2,1,0:T(8,128)(2,1)}, u32[]{:S(2)}) copy-start(bf16[2,32,16,128]{3,2,1,0:T(8,128)(2,1)} %param.16) | copy-start | bytes 786436
  0.6 40.2 %copy-start.2 = (bf16[128,1024]{1,0:T(8,128)(2,1)S(1)}, bf16[128,1024]{1,0:T(8,128)(2,1)}, u32[]{:S(2)}) copy-start(bf16[128,1024]{1,0:T(8,128)(2,1)} %param.14) | copy-start | bytes 786436
  0.7 40.2 %copy-start.19 = (f32[128]{0:T(128)S(1)}, f32[128]{0:T(128)}, u32[]{:S(2)}) copy-start(f32[128]{0:T(128)} %param.13) | copy-start | bytes 1540
  0.7 40.4 %copy-start.8 = (bf16[256,1024]{1,0:T(8,128)(2,1)S(1)}, bf16[256,1024]{1,0:T(8,128)(2,1)}, u32[]{:S(2)}) copy-start(bf16[256,1024]{1,0:T(8,128)(2,1)} %param.12) | copy-start | bytes 1572868
  0.7 40.5 %copy-start.13 = (bf16[2,128,128]{2,1,0:T(8,128)(2,1)S(1)}, bf16[2,128,128]{2,1,0:T(8,128)(2,1)}, u32[]{:S(2)}) copy-start(bf16[2,128,128]{2,1,0:T(8,128)(2,1)} %param.15) | copy-start | bytes 196612
  29.8 156.8 %copy-start.20 = (s32[32]{0:T(128)S(1)}, s32[32]{0:T(128)}, u32[]{:S(2)}) copy-start(s32[32]{0:T(128)} %param.19) | copy-start | bytes 388
  29.8 158.2 %copy-start.12 = (bf16[2,256,128]{2,1,0:T(8,128)(2,1)S(1)}, bf16[2,256,128]{2,1,0:T(8,128)(2,1)}, u32[]{:S(2)}) copy-start(bf16[2,256,128]{2,1,0:T(8,128)(2,1)} %param.11) | copy-start | bytes 393220
  31.3 157.4 %copy-start.5 = (bf16[256,1024]{1,0:T(8,128)(2,1)S(1)}, bf16[256,1024]{1,0:T(8,128)(2,1)}, u32[]{:S(2)}) copy-start(bf16[256,1024]{1,0:T(8,128)(2,1)} %param.10) | copy-start | bytes 1572868
  31.3 158.8 %all-to-all-start = ((bf16[2,1,64,16,128]{4,3,0,1,2:T(8,128)(2,1)}), bf16[2,1,64,16,128]{4,3,0,1,2:T(8,128)(2,1)S(1)}, u32[]{:S(2)}, u32[]{:S(2)}) async-start(bf16[2,1,64,16,128]{4,3,0,1,2:T(8,128)(2,1)} %bitcast.7), calls=%async_computation | async-start | bytes 1048576 | tf_op jit(solution)/shard_map/all_to_all | solution.py:117
  186.6 3.5 copy-start.15
  187.9 4.1 %copy-start.17 = (pred[1024]{0:T(1024)(128)(4,1)}, pred[1024]{0:T(1024)(128)(4,1)S(1)}, u32[]{:S(2)}) copy-start(pred[1024]{0:T(1024)(128)(4,1)S(1)} %iota_compare_fusion.1) | copy-start | bytes 3076
  188.0 3.5 copy-start.9
  190.1 1.4 copy-start.4
  190.1 4.8 %copy-start.11 = (bf16[1,1,64,16,128]{4,3,0,1,2:T(8,128)(2,1)}, bf16[1,1,64,16,128]{4,3,0,1,2:T(8,128)(2,1)S(1)}, u32[]{:S(2)}) copy-start(bf16[1,1,64,16,128]{4,3,0,1,2:T(8,128)(2,1)S(1)} %get-tuple-element.57) | copy-start | bytes 786436
  191.5 3.4 copy-start.1
  192.0 2.3 copy-start.7
  192.0 2.3 copy-start.10
  194.3 0.7 copy-start.18
  207.1 1.9 copy-start.6
  207.2 1.9 copy-start.16
  209.6 146.2 %copy-start.3 = (bf16[128,1024]{1,0:T(8,128)(2,1)S(1)}, bf16[128,1024]{1,0:T(8,128)(2,1)}, u32[]{:S(2)}) copy-start(bf16[128,1024]{1,0:T(8,128)(2,1)} %param.14) | copy-start | bytes 786436
  210.3 145.8 %copy-start.14 = (bf16[2,128,128]{2,1,0:T(8,128)(2,1)S(1)}, bf16[2,128,128]{2,1,0:T(8,128)(2,1)}, u32[]{:S(2)}) copy-start(bf16[2,128,128]{2,1,0:T(8,128)(2,1)} %param.15) | copy-start | bytes 196612
where the time goes:
time: 376 us; the launch traced here: 373 us
  blocking collectives  331 us (88%)
  matrix products  20 us (5%)
  starting transfers between devices  8.91 us (2%)
  local copies, waits for them, and re-layouts  5.73 us (2%)
  other arithmetic  5.61 us (1%)
    psum x1, blocking collectives, shards(): shift_q, shift_kv = lax.psum((part_q, part_kv), 'dp')  144 us
    psum x1, blocking collectives, shards(): lax.psum((jnp.sum(query_full, 0), jnp.sum(kv_full, 1)), 'dp')  143 us
    unnamed x1, blocking collectives  26.3 us
    psum x1, blocking collectives, shards(): steer_grad = lax.psum(steer_part, 'tensor')  17 us
    all_to_all x1, starting transfers between devices, shards(): lax.all_to_all(outgoing, 'dp', split_axis=2, concat_axis=2, tiled=True)  8.91 us
  transfers between devices with their start and end apart: 1, of which 0 were waited for; matrix products, arithmetic and copies ran while one was open for 1% of the time, Pallas kernels for 0%

commit v1 on v0

v1 whole, which is shorter than its diff:
```python
import functools
import math

import jax
import jax.numpy as jnp
from jax import lax
from jax.experimental import pallas as pl
from jax.experimental.pallas import tpu as pltpu
from jax.sharding import PartitionSpec as P

HD = 128
NN = (((1,), (0,)), ((), ()))
NT = (((1,), (1,)), ((), ()))
TN = (((0,), (0,)), ((), ()))
VMEM = pl.BlockSpec(memory_space=pltpu.VMEM)
SMEM = pl.BlockSpec(memory_space=pltpu.SMEM)
PARAMS = pltpu.CompilerParams(vmem_limit_bytes=40 * 2**20)


def dot(a, b, dims):
    return lax.dot_general(a, b, dims, preferred_element_type=jnp.float32)


def in_thirds(row):
    first = row.astype(jnp.bfloat16).astype(jnp.float32)
    second = (row - first).astype(jnp.bfloat16).astype(jnp.float32)
    third = row - first - second
    rest = jnp.zeros((13, row.shape[1]), jnp.float32)
    return jnp.concatenate([first, second, third, rest], axis=0).astype(jnp.bfloat16)


def project_kernel(prompt_id, steering, w_query, w_kv, message):
    thirds = in_thirds(steering[...])
    parts = [
        jnp.sum(dot(thirds, weights, NN), 0, keepdims=True)
        for weights in (w_query[...], w_kv[0], w_kv[1])
    ]
    mark = jnp.full((1, HD), prompt_id[0], jnp.int32).astype(jnp.float32)
    row = jnp.concatenate(parts + [mark], axis=1)
    for peer in range(message.shape[0]):
        message[peer] = row


def pick_kernel(ids, cache, outgoing):
    def one(peer, carry):
        outgoing[peer] = cache[:, ids[peer]]
        return carry

    lax.fori_loop(0, outgoing.shape[0], one, 0, unroll=4)


def attend_kernel(
    ids,
    lens,
    prompt_lens,
    arrived,
    q_ref,
    kv_ref,
    cot_ref,
    shifts,
    dq_ref,
    dkv_ref,
    message,
    keys,
    values,
    grad_keys,
    grad_values,
    sums,
):
    span = arrived.shape[0] * arrived.shape[2]
    own = kv_ref.shape[1]
    heads = q_ref.shape[1] // HD
    scale = 1.0 / math.sqrt(HD)
    to_log2 = scale * math.log2(math.e)
    live = lens[0]
    prompt_live = prompt_lens[ids[0]]
    total = shifts[0]
    for peer in range(1, shifts.shape[0]):
        total = total + shifts[peer]

    def shift_of(chunk):
        return total[:, chunk * HD : (chunk + 1) * HD]

    for head in range(heads):
        sums[head] = shift_of(head)
    keys[:span] = arrived[:, 0].reshape(span, HD)
    values[:span] = arrived[:, 1].reshape(span, HD)
    keys[span:] = (kv_ref[0].astype(jnp.float32) + shift_of(heads)).astype(jnp.bfloat16)
    values[span:] = (kv_ref[1].astype(jnp.float32) + shift_of(heads + 1)).astype(jnp.bfloat16)
    grad_keys[...] = jnp.zeros_like(grad_keys)
    grad_values[...] = jnp.zeros_like(grad_values)

    def one_head(head, carry):
        columns = pl.ds(pl.multiple_of(head * HD, HD), HD)
        query = (q_ref[:, columns].astype(jnp.float32) + sums[head]).astype(jnp.bfloat16)
        token = lax.broadcasted_iota(jnp.int32, (own, HD), 0)
        grad = cot_ref[:, columns].astype(jnp.float32)
        grad = jnp.where(token < live, grad, 0.0).astype(jnp.bfloat16)
        scores = dot(query, keys[...], NT)
        place = lax.broadcasted_iota(jnp.int32, (own, span), 1)
        pre = jnp.where(place < prompt_live, scores[:, :span], -jnp.inf)
        key_at = lax.broadcasted_iota(jnp.int32, (own, own), 1)
        token_at = lax.broadcasted_iota(jnp.int32, (own, own), 0)
        admitted = (key_at <= token_at) & (key_at < live)
        mine = jnp.where(admitted, scores[:, span:], -jnp.inf)
        top = jnp.maximum(jnp.max(pre, 1, keepdims=True), jnp.max(mine, 1, keepdims=True))
        top = top * to_log2
        pre = jnp.exp2(pre * to_log2 - top)
        mine = jnp.exp2(mine * to_log2 - top)
        mass = jnp.sum(pre, 1, keepdims=True) + jnp.sum(mine, 1, keepdims=True)
        grad_weights = dot(grad, values[...], NT)
        pre_gw, mine_gw = grad_weights[:, :span], grad_weights[:, span:]
        inverse = 1.0 / mass
        delta = jnp.sum(pre * pre_gw, 1, keepdims=True) + jnp.sum(mine * mine_gw, 1, keepdims=True)
        slope = scale * inverse
        offset = delta * inverse * slope
        pre_gs = (pre * (pre_gw * slope - offset)).astype(jnp.bfloat16)
        mine_gs = (mine * (mine_gw * slope - offset)).astype(jnp.bfloat16)
        weights = (mine * inverse).astype(jnp.bfloat16)
        grad_query = dot(pre_gs, keys[:span], NN) + dot(mine_gs, keys[span:], NN)
        dq_ref[:, columns] = grad_query.astype(jnp.bfloat16)
        grad_keys[...] += dot(mine_gs, query, TN)
        grad_values[...] += dot(weights, grad, TN)
        sums[head] = jnp.sum(grad_query, 0, keepdims=True)
        return carry

    lax.fori_loop(0, heads, one_head, 0)
    dkv_ref[0] = grad_keys[...].astype(jnp.bfloat16)
    dkv_ref[1] = grad_values[...].astype(jnp.bfloat16)
    row = jnp.concatenate(
        [sums[head] for head in range(heads)]
        + [jnp.sum(grad_keys[...], 0, keepdims=True), jnp.sum(grad_values[...], 0, keepdims=True)],
        axis=1,
    )
    for peer in range(message.shape[0]):
        message[peer] = row


def steer_kernel(sums, w_query, w_kv, message):
    total = sums[0]
    for peer in range(1, sums.shape[0]):
        total = total + sums[peer]
    wide = w_query.shape[1]
    part = dot(in_thirds(total[:, :wide]), w_query[...], NT)
    for c in range(2):
        chunk = total[:, wide + c * HD : wide + (c + 1) * HD]
        part = part + dot(in_thirds(chunk), w_kv[c], NT)
    row = jnp.sum(part, 0, keepdims=True)
    for peer in range(message.shape[0]):
        message[peer] = row


def shards(
    q_base,
    kv_base,
    cotangent,
    steering,
    w_query,
    w_kv,
    prompt_cache,
    prompt_ids,
    dialogue_lens,
    prompt_lens,
):
    dp = lax.axis_size("dp")
    tensor = lax.axis_size("tensor")
    f32 = jnp.float32
    tokens, width = q_base.shape
    positions = prompt_cache.shape[2]
    all_width = width + 2 * HD
    message = pl.pallas_call(
        project_kernel,
        out_shape=jax.ShapeDtypeStruct((dp, 1, all_width + HD), f32),
        in_specs=[SMEM, VMEM, VMEM, VMEM],
        out_specs=VMEM,
        compiler_params=PARAMS,
        name="project",
    )(prompt_ids, steering.reshape(1, -1), w_query, w_kv)
    shares = lax.all_to_all(message, "dp", 0, 0, tiled=True)
    ids = shares[:, 0, all_width].astype(jnp.int32)
    outgoing = pl.pallas_call(
        pick_kernel,
        out_shape=jax.ShapeDtypeStruct((dp, 2, positions, HD), jnp.bfloat16),
        in_specs=[SMEM, VMEM],
        out_specs=VMEM,
        compiler_params=PARAMS,
        name="pick",
    )(ids, prompt_cache)
    arrived = lax.all_to_all(outgoing, "dp", 0, 0, tiled=True)
    keys_held = dp * positions + tokens
    query_grad, kv_grad, message = pl.pallas_call(
        attend_kernel,
        out_shape=(
            jax.ShapeDtypeStruct(q_base.shape, jnp.bfloat16),
            jax.ShapeDtypeStruct(kv_base.shape, jnp.bfloat16),
            jax.ShapeDtypeStruct((dp, 1, all_width), f32),
        ),
        in_specs=[SMEM, SMEM, SMEM, VMEM, VMEM, VMEM, VMEM, VMEM],
        out_specs=(VMEM, VMEM, VMEM),
        scratch_shapes=[
            pltpu.VMEM((keys_held, HD), jnp.bfloat16),
            pltpu.VMEM((keys_held, HD), jnp.bfloat16),
            pltpu.VMEM((tokens, HD), f32),
            pltpu.VMEM((tokens, HD), f32),
            pltpu.VMEM((width // HD, 1, HD), f32),
        ],
        compiler_params=PARAMS,
        name="attend",
    )(prompt_ids, dialogue_lens, prompt_lens, arrived, q_base, kv_base, cotangent, shares)
    sums = lax.all_to_all(message, "dp", 0, 0, tiled=True)
    message = pl.pallas_call(
        steer_kernel,
        out_shape=jax.ShapeDtypeStruct((tensor, 1, steering.shape[0]), f32),
        in_specs=[VMEM, VMEM, VMEM],
        out_specs=VMEM,
        compiler_params=PARAMS,
        name="steer",
    )(sums, w_query, w_kv)
    parts = lax.all_to_all(message, "tensor", 0, 0, tiled=True)
    return (query_grad, kv_grad, jnp.sum(parts, axis=(0, 1)))


def solution(mesh):
    placed = (
        P("dp", "tensor"),
        P(None, "dp", "tensor"),
        P("dp", "tensor"),
        P("dp"),
        P("dp", "tensor"),
        P(None, "dp", "tensor"),
        P(None, None, "dp", "tensor"),
        P("dp"),
        P("dp"),
        P(),
    )
    return jax.shard_map(
        shards,
        mesh=mesh,
        in_specs=placed,
        out_specs=(P("dp", "tensor"), P(None, "dp", "tensor"), P("dp")),
        check_vma=False,
    )
```

time: 376 us -> 109 us (0.29)
  blocking collectives: 331 us -> 63.5 us
  matrix products: 20 us -> 0 us
  waiting for transfers between devices: 0.01 us -> 18.8 us
  Pallas kernels: 0 us -> 12.7 us
  other arithmetic: 5.61 us -> 1.76 us
    psum x3 -> x0, blocking collectives: 304 us -> none  [the longest x1 144 us: shards(): shift_q, shift_kv = lax.psum((part_q, part_kv), 'dp')]
    all_to_all x0 -> x3, blocking collectives: none -> 63.5 us  [the longest x1 32.9 us: shards(): shares = lax.all_to_all(message, 'dp', 0, 0, tiled=True)]
    unnamed x1 -> x0, blocking collectives: 26.3 us -> none
    dot_general x13 -> x0, matrix products: 20 us -> none  [the longest x1 7.5 us: backward_of(): jnp.einsum('tgp,pd->tgd', pre_gs, pre_keys, preferred_element_type=jnp.fl...]
    all_to_all x1, waiting for transfers between devices: 0.01 us -> 18.8 us  [shards(): arrived = lax.all_to_all(outgoing, 'dp', 0, 0, tiled=True)]
    pallas_call x0 -> x4, Pallas kernels: none -> 12.7 us  [the longest x1 10.7 us: shards(): pl.pallas_call(attend_kernel, out_shape=(jax.ShapeDtypeStruct(q_base.shap...]
  transfers between devices with their start and end apart: 1 -> 1, of which waited for: 0 -> 1; matrix products, arithmetic and copies ran while one was open for 1% -> 0% of each run, Pallas kernels for 0% -> 0%
where the time goes in v1:
time: 109 us
  blocking collectives  63.5 us (58%)
  waiting for transfers between devices  18.8 us (17%)
  Pallas kernels  12.7 us (12%)
  starting transfers between devices  7.4 us (7%)
  local copies, waits for them, and re-layouts  2.47 us (2%)
  between operations  2.02 us (2%)
  other arithmetic  1.76 us (2%)
    all_to_all x1, blocking collectives, shards(): shares = lax.all_to_all(message, 'dp', 0, 0, tiled=True)  32.9 us
    all_to_all x1, blocking collectives, shards(): sums = lax.all_to_all(message, 'dp', 0, 0, tiled=True)  21.7 us
    all_to_all x1, waiting for transfers between devices, shards(): arrived = lax.all_to_all(outgoing, 'dp', 0, 0, tiled=True)  18.8 us
    pallas_call x1, Pallas kernels, shards(): pl.pallas_call(attend_kernel, out_shape=(jax.ShapeDtypeStruct(q_base.shap...  10.7 us
    all_to_all x1, blocking collectives, shards(): parts = lax.all_to_all(message, 'tensor', 0, 0, tiled=True)  8.85 us
    all_to_all x1, starting transfers between devices, shards(): arrived = lax.all_to_all(outgoing, 'dp', 0, 0, tiled=True)  7.4 us
    unnamed x20, local copies, waits for them, and re-layouts  2.47 us
  transfers between devices with their start and end apart: 1, of which 1 were waited for; matrix products, arithmetic and copies ran while one was open for 0% of the time, Pallas kernels for 0%

profile of v1, /device:TPU:1, one launch (start us, length us, event | category | flops | bytes accessed | tf_op | source)
XLA Modules:
  0.0 108.6 jit_solution(12615482098679098749)
XLA Ops:
  1.3 0.0 copy-start.8
  1.3 0.6 copy-done.8
  1.9 0.0 copy-start
  1.9 0.9 copy-done
  2.9 0.0 copy-start.5
  2.9 0.8 copy-done.5
  3.7 0.2 project.1
  3.9 0.0 copy-start.4
  3.9 32.9 %all_to_all.20.shifts = f32[64,1,1408]{2,1,0:T(1,128)S(1)} all-to-all(f32[64,1,1408]{2,1,0:T(1,128)S(1)} %project.1), channel_id=1, replica_groups=mesh['dp'=64,'tensor'=8] {'dp'}, dimensions={0} | all-to-all | bytes 720896 | tf_op jit(solution)/shard_map/all_to_all | solution.py:179
  36.8 1.2 %fusion.ids = s32[64]{0:T(128)S(1)} fusion(f32[64,1,1408]{2,1,0:T(1,128)S(1)} %all_to_all.20.shifts), kind=kLoop, calls=%fused_computation.1 | loop fusion | flops 64 | bytes 512 | tf_op jit(solution)/shard_map/convert_element_type | solution.py:180
  38.1 0.0 copy-done.4
  38.1 0.0 copy-start.7
  38.1 1.5 %pick.1 = bf16[64,2,16,128]{3,2,1,0:T(8,128)(2,1)} custom-call(s32[64]{0:T(128)S(1)} %fusion.ids, bf16[2,32,16,128]{3,2,1,0:T(8,128)(2,1)S(1)} %copy-done.4), custom_call_target="tpu_custom_call" | custom-call | tf_op jit(solution)/shard_map/pick/pallas_call | solution.py:181
  39.6 0.0 copy-start.2
  39.6 0.0 copy-start.3
  39.6 7.4 %all-to-all-start.1 = ((bf16[64,2,16,128]{3,2,1,0:T(8,128)(2,1)}), bf16[64,2,16,128]{3,2,1,0:T(8,128)(2,1)S(1)}, u32[]{:S(2)}, u32[]{:S(2)}) async-start(bf16[64,2,16,128]{3,2,1,0:T(8,128)(2,1)} %pick.1), calls=%async_computation.1 | async-start | bytes 1048576 | tf_op jit(solution)/shard_map/all_to_all | solution.py:189
  47.0 0.0 copy-start.9
  47.7 18.8 %all-to-all-done.1.arrived = bf16[64,2,16,128]{3,2,1,0:T(8,128)(2,1)S(1)} async-done(((bf16[64,2,16,128]{3,2,1,0:T(8,128)(2,1)}), bf16[64,2,16,128]{3,2,1,0:T(8,128)(2,1)S(1)}, u32[]{:S(2)}, u32[]{:S(2)}) %all-to-all-start.1) | async-done | bytes 524320 | tf_op jit(solution)/shard_map/all_to_all | solution.py:189
  66.5 0.0 copy-done.7
  66.5 0.0 copy-done.2
  66.5 0.0 copy-done.3
  66.5 0.0 copy-done.9
  66.5 10.7 %attend.1 = (bf16[256,1024]{1,0:T(8,128)(2,1)}, bf16[2,256,128]{2,1,0:T(8,128)(2,1)}, f32[64,1,1280]{2,1,0:T(1,128)S(1)}) custom-call(s32[1]{0:T(128)S(6)} %copy.13.prompt_id.ids, s32[1]{0:T(128)S(6)} %copy.14.lens, s32[32]{0:T(128)S(1)} %copy-done.9, bf16[64,2,16,128]{3,2,1,0:T(8,128)(2,1)S(1)} %all-to-all-done.1.arrived, bf16[256,1024]{1,0:T(8,128)(2,1)S(1)} %copy-done.2, ...), custom_call_target="tpu_custom_call" | custom-call | tf_op jit(solution)/shard_map/attend/pallas_call | solution.py:191
  77.2 0.0 copy-start.1
  77.2 0.0 copy-start.6
  77.2 21.7 %all_to_all.21.sums = f32[64,1,1280]{2,1,0:T(1,128)S(1)} all-to-all(f32[64,1,1280]{2,1,0:T(1,128)S(1)} %get-tuple-element.8), channel_id=1, replica_groups=mesh['dp'=64,'tensor'=8] {'dp'}, dimensions={0} | all-to-all | bytes 655360 | tf_op jit(solution)/shard_map/all_to_all | solution.py:210
  98.9 0.0 copy-done.1
  98.9 0.0 copy-done.6
  98.9 0.3 steer.1
  99.2 8.8 %all_to_all.22 = f32[8,1,128]{2,1,0:T(1,128)S(1)} all-to-all(f32[8,1,128]{2,1,0:T(1,128)S(1)} %steer.1), channel_id=1, replica_groups=mesh['dp'=64,'tensor'=8] {'tensor'}, dimensions={0} | all-to-all | bytes 8192 | tf_op jit(solution)/shard_map/all_to_all | solution.py:219
  108.1 0.5 reduce_sum.9
Async XLA Ops:
  1.3 0.7 copy-start.8
  1.9 0.9 copy-start
  2.9 0.8 copy-start.5
  3.9 34.1 %copy-start.4 = (bf16[2,32,16,128]{3,2,1,0:T(8,128)(2,1)S(1)}, bf16[2,32,16,128]{3,2,1,0:T(8,128)(2,1)}, u32[]{:S(2)}) copy-start(bf16[2,32,16,128]{3,2,1,0:T(8,128)(2,1)} %cache.1) | copy-start | bytes 786436
  38.1 28.4 %copy-start.7 = (bf16[2,256,128]{2,1,0:T(8,128)(2,1)S(1)}, bf16[2,256,128]{2,1,0:T(8,128)(2,1)}, u32[]{:S(2)}) copy-start(bf16[2,256,128]{2,1,0:T(8,128)(2,1)} %kv_ref.1) | copy-start | bytes 393220
  39.6 26.9 %copy-start.2 = (bf16[256,1024]{1,0:T(8,128)(2,1)S(1)}, bf16[256,1024]{1,0:T(8,128)(2,1)}, u32[]{:S(2)}) copy-start(bf16[256,1024]{1,0:T(8,128)(2,1)} %q_ref.1) | copy-start | bytes 1572868
  39.6 26.9 %copy-start.3 = (bf16[256,1024]{1,0:T(8,128)(2,1)S(1)}, bf16[256,1024]{1,0:T(8,128)(2,1)}, u32[]{:S(2)}) copy-start(bf16[256,1024]{1,0:T(8,128)(2,1)} %cot_ref.1) | copy-start | bytes 1572868
  39.6 26.9 %all-to-all-start.1 = ((bf16[64,2,16,128]{3,2,1,0:T(8,128)(2,1)}), bf16[64,2,16,128]{3,2,1,0:T(8,128)(2,1)S(1)}, u32[]{:S(2)}, u32[]{:S(2)}) async-start(bf16[64,2,16,128]{3,2,1,0:T(8,128)(2,1)} %pick.1), calls=%async_computation.1 | async-start | bytes 1048576 | tf_op jit(solution)/shard_map/all_to_all | solution.py:189
  47.0 19.5 %copy-start.9 = (s32[32]{0:T(128)S(1)}, s32[32]{0:T(128)}, u32[]{:S(2)}) copy-start(s32[32]{0:T(128)} %prompt_lens.1) | copy-start | bytes 388
  77.2 21.7 %copy-start.1 = (bf16[128,1024]{1,0:T(8,128)(2,1)S(1)}, bf16[128,1024]{1,0:T(8,128)(2,1)}, u32[]{:S(2)}) copy-start(bf16[128,1024]{1,0:T(8,128)(2,1)} %w_query.3) | copy-start | bytes 786436
  77.2 21.7 %copy-start.6 = (bf16[2,128,128]{2,1,0:T(8,128)(2,1)S(1)}, bf16[2,128,128]{2,1,0:T(8,128)(2,1)}, u32[]{:S(2)}) copy-start(bf16[2,128,128]{2,1,0:T(8,128)(2,1)} %w_kv.3) | copy-start | bytes 196612

commit v2 on v1

v2 whole, which is shorter than its diff:
```python
import functools
import math

import jax
import jax.numpy as jnp
from jax import lax
from jax.experimental import pallas as pl
from jax.experimental.pallas import tpu as pltpu
from jax.sharding import PartitionSpec as P

HD = 128
ROWS = 16
MASKED = -1e30
NN = (((1,), (0,)), ((), ()))
NT = (((1,), (1,)), ((), ()))
TN = (((0,), (0,)), ((), ()))
VMEM = pl.BlockSpec(memory_space=pltpu.VMEM)
HBM = pl.BlockSpec(memory_space=pltpu.HBM)
SMEM = pl.BlockSpec(memory_space=pltpu.SMEM)
PARAMS = pltpu.CompilerParams(vmem_limit_bytes=40 * 2**20)


def dot(a, b, dims):
    return lax.dot_general(a, b, dims, preferred_element_type=jnp.float32)


def in_thirds(row):
    first = row.astype(jnp.bfloat16).astype(jnp.float32)
    second = (row - first).astype(jnp.bfloat16).astype(jnp.float32)
    third = row - first - second
    rest = jnp.zeros((13, row.shape[1]), jnp.float32)
    return jnp.concatenate([first, second, third, rest], axis=0).astype(jnp.bfloat16)


def in_halves(chunks):
    half = len(chunks) // 2
    rows = [jnp.concatenate(chunks[:half], axis=1), jnp.concatenate(chunks[half:], axis=1)]
    return jnp.concatenate(rows, axis=0).astype(jnp.bfloat16)


def summed(blocks):
    total = blocks[0].astype(jnp.float32)
    for peer in range(1, blocks.shape[0]):
        total = total + blocks[peer].astype(jnp.float32)
    return total


def chunk_of(halves, chunk, count):
    row, at = divmod(chunk, count // 2)
    return halves[row : row + 1, at * HD : (at + 1) * HD]


def project_kernel(prompt_id, steering, w_query, w_kv, message, vector, wq, wkv, sems):
    copies = [
        pltpu.make_async_copy(source, held, sems.at[at])
        for at, (source, held) in enumerate(((w_query, wq), (steering, vector), (w_kv, wkv)))
    ]
    for copy in copies:
        copy.start()
    mark = jnp.full((1, HD), prompt_id[0], jnp.int32).astype(jnp.float32)
    for copy in copies:
        copy.wait()
    thirds = in_thirds(vector[...])
    parts = [jnp.sum(dot(thirds, w[...], NN), 0, keepdims=True) for w in (wq, wkv.at[0], wkv.at[1])]
    row = jnp.concatenate(parts, axis=1)
    chunks = [row[:, at : at + HD] for at in range(0, row.shape[1], HD)]
    half = len(chunks) // 2
    block = in_halves(chunks[:half] + [mark] + chunks[half:] + [mark])
    for peer in range(message.shape[0]):
        message[peer] = block


def pick_kernel(shares, cache, outgoing, marks, ids, sems):
    peers = shares.shape[0]
    last = shares.shape[2] - HD
    lane = lax.broadcasted_iota(jnp.int32, (2, HD), 1)
    found = jnp.zeros((2, HD), jnp.float32)
    for peer in range(peers):
        found = jnp.where(lane == peer, shares[peer, :, last:].astype(jnp.float32), found)
    marks[...] = found[:1].astype(jnp.int32)
    copy = pltpu.make_async_copy(marks, ids, sems.at[0])
    copy.start()
    copy.wait()
    for peer in range(peers):
        pltpu.make_async_copy(cache.at[:, ids[0, peer]], outgoing.at[peer], sems.at[1]).start()
    pltpu.make_async_copy(outgoing, outgoing, sems.at[1]).wait()


def attend_kernel(
    ids,
    lens,
    prompt_lens,
    arrived,
    q_ref,
    kv_ref,
    cot_ref,
    shifts,
    dq_ref,
    dkv_ref,
    message,
    keys,
    keys_t,
    values_t,
    grad_keys,
    grad_values,
    causal,
    scores0,
    scores1,
    slopes0,
    slopes1,
    grads0,
    grads1,
    weights0,
    weights1,
    queries0,
    queries1,
    outs0,
    outs1,
    factors0,
    factors1,
):
    f32, bf16 = jnp.float32, jnp.bfloat16
    span = arrived.shape[0] * arrived.shape[2]
    own = kv_ref.shape[1]
    heads = q_ref.shape[1] // HD
    scale = 1.0 / math.sqrt(HD)
    to_log2 = scale * math.log2(math.e)
    live = lens[0]
    prompt_live = prompt_lens[ids[0]]
    total = summed(shifts)
    shift = [chunk_of(total[:, : total.shape[1] - HD], c, heads + 2) for c in range(heads + 2)]
    pre_keys = arrived[:, 0].reshape(span, HD)
    pre_values = arrived[:, 1].reshape(span, HD)
    own_keys = (kv_ref[0].astype(f32) + shift[heads]).astype(bf16)
    own_values = (kv_ref[1].astype(f32) + shift[heads + 1]).astype(bf16)
    keys[:span] = pre_keys
    keys[span:] = own_keys
    keys_t[:HD, :span] = pre_keys.T
    keys_t[:HD, span:] = own_keys.T
    values_t[:, :span] = pre_values.T
    values_t[:, span:] = own_values.T
    feature = lax.broadcasted_iota(jnp.int32, (HD, span + own), 0)
    place = lax.broadcasted_iota(jnp.int32, (HD, span + own), 1)
    barred = jnp.where((place >= prompt_live) & (place < span), MASKED, 0.0)
    keys_t[HD:] = jnp.where(feature == HD - 1, barred, keys_t[:HD].astype(f32)).astype(bf16)
    token_at = lax.broadcasted_iota(jnp.int32, (own, own), 0)
    key_at = lax.broadcasted_iota(jnp.int32, (own, own), 1)
    causal[...] = jnp.where((key_at <= token_at) & (key_at < live), 0.0, MASKED)
    grad_keys[...] = jnp.zeros_like(grad_keys)
    grad_values[...] = jnp.zeros_like(grad_values)
    token = lax.broadcasted_iota(jnp.int32, (own, HD), 0)
    lane = lax.broadcasted_iota(jnp.int32, (own, HD), 1)
    scores, slopes = (scores0, scores1), (slopes0, slopes1)
    grads, weights = (grads0, grads1), (weights0, weights1)
    queries, outs, factors = (queries0, queries1), (outs0, outs1), (factors0, factors1)
    sums = []

    def products(head):
        slot, columns = head % 2, slice(head * HD, (head + 1) * HD)
        query = (q_ref[:, columns].astype(f32) + shift[head]).astype(bf16)
        grad = jnp.where(token < live, cot_ref[:, columns].astype(f32), 0.0).astype(bf16)
        queries[slot][...] = query
        outs[slot][...] = grad
        scaled = query.astype(f32) * to_log2
        high = scaled.astype(bf16)
        low = jnp.where(lane == HD - 1, 1.0, scaled - high.astype(f32)).astype(bf16)
        scores[slot][...] = dot(jnp.concatenate([high, low], axis=1), keys_t[...], NN)
        slopes[slot][...] = dot(grad, values_t[...], NN)

    def softmax(head):
        slot = head % 2
        for at in range(0, own, ROWS):
            rows = slice(at, at + ROWS)
            score = scores[slot][rows]
            score = jnp.concatenate([score[:, :span], score[:, span:] + causal[rows]], axis=1)
            prob = jnp.exp2(score - jnp.max(score, 1, keepdims=True))
            slope = slopes[slot][rows]
            inverse = 1.0 / jnp.sum(prob, 1, keepdims=True)
            delta = jnp.sum(prob * slope, 1, keepdims=True) * inverse
            grads[slot][rows] = (prob * (slope - delta)).astype(bf16)
            weights[slot][rows] = (prob[:, span:] * inverse).astype(bf16)
            factors[slot][rows] = jnp.broadcast_to(inverse * scale, (ROWS, HD))

    def gradients(head):
        slot, columns = head % 2, slice(head * HD, (head + 1) * HD)
        factor = factors[slot][...]
        grad_query = dot(grads[slot][...], keys[...], NN) * factor
        dq_ref[:, columns] = grad_query.astype(bf16)
        sums.append(jnp.sum(grad_query, 0, keepdims=True))
        query = (queries[slot][...].astype(f32) * factor).astype(bf16)
        grad_keys[...] += dot(grads[slot][:, span:], query, TN)
        grad_values[...] += dot(weights[slot][...], outs[slot][...], TN)

    products(0)
    for head in range(heads):
        if head > 0:
            gradients(head - 1)
        if head + 1 < heads:
            products(head + 1)
        softmax(head)
    gradients(heads - 1)
    dkv_ref[0] = grad_keys[...].astype(bf16)
    dkv_ref[1] = grad_values[...].astype(bf16)
    last = [jnp.sum(grad_keys[...], 0, keepdims=True), jnp.sum(grad_values[...], 0, keepdims=True)]
    block = in_halves(sums + last)
    for peer in range(message.shape[0]):
        message[peer] = block


def steer_kernel(sums, w_query, w_kv, message):
    total = summed(sums)
    heads = w_query.shape[1] // HD
    chunks = [chunk_of(total, chunk, heads + 2) for chunk in range(heads + 2)]
    part = dot(in_thirds(jnp.concatenate(chunks[:heads], axis=1)), w_query[...], NT)
    for c in range(2):
        part = part + dot(in_thirds(chunks[heads + c]), w_kv[c], NT)
    row = jnp.sum(part, 0, keepdims=True)
    for peer in range(message.shape[0]):
        message[peer] = row


def shards(
    q_base,
    kv_base,
    cotangent,
    steering,
    w_query,
    w_kv,
    prompt_cache,
    prompt_ids,
    dialogue_lens,
    prompt_lens,
):
    dp = lax.axis_size("dp")
    tensor = lax.axis_size("tensor")
    f32 = jnp.float32
    tokens, width = q_base.shape
    positions = prompt_cache.shape[2]
    half_width = (width + 2 * HD) // 2
    bf16 = jnp.bfloat16
    message = pl.pallas_call(
        project_kernel,
        out_shape=jax.ShapeDtypeStruct((dp, 2, half_width + HD), bf16),
        in_specs=[SMEM, HBM, HBM, HBM],
        out_specs=VMEM,
        scratch_shapes=[
            pltpu.VMEM((1, steering.shape[0]), f32),
            pltpu.VMEM(w_query.shape, bf16),
            pltpu.VMEM(w_kv.shape, bf16),
            pltpu.SemaphoreType.DMA((3,)),
        ],
        compiler_params=pltpu.CompilerParams(vmem_limit_bytes=63 * 2**20),
        name="project",
    )(prompt_ids, steering.reshape(1, -1), w_query, w_kv)
    shares = lax.all_to_all(message, "dp", 0, 0, tiled=True)
    outgoing = pl.pallas_call(
        pick_kernel,
        out_shape=jax.ShapeDtypeStruct((dp, 2, positions, HD), bf16),
        in_specs=[VMEM, VMEM],
        out_specs=HBM,
        scratch_shapes=[
            pltpu.VMEM((1, HD), jnp.int32),
            pltpu.SMEM((1, HD), jnp.int32),
            pltpu.SemaphoreType.DMA((2,)),
        ],
        compiler_params=PARAMS,
        name="pick",
    )(shares, prompt_cache)
    arrived = lax.all_to_all(outgoing, "dp", 0, 0, tiled=True)
    keys_held = dp * positions + tokens
    query_grad, kv_grad, message = pl.pallas_call(
        attend_kernel,
        out_shape=(
            jax.ShapeDtypeStruct(q_base.shape, jnp.bfloat16),
            jax.ShapeDtypeStruct(kv_base.shape, jnp.bfloat16),
            jax.ShapeDtypeStruct((dp, 2, half_width), bf16),
        ),
        in_specs=[SMEM, SMEM, SMEM, VMEM, VMEM, VMEM, VMEM, VMEM],
        out_specs=(VMEM, VMEM, VMEM),
        scratch_shapes=[
            pltpu.VMEM((keys_held, HD), bf16),
            pltpu.VMEM((2 * HD, keys_held), bf16),
            pltpu.VMEM((HD, keys_held), bf16),
            pltpu.VMEM((tokens, HD), f32),
            pltpu.VMEM((tokens, HD), f32),
            pltpu.VMEM((tokens, tokens), f32),
        ]
        + [
            pltpu.VMEM((tokens, columns), kind)
            for columns, kind in (
                (keys_held, f32),
                (keys_held, f32),
                (keys_held, bf16),
                (tokens, bf16),
                (HD, bf16),
                (HD, bf16),
                (HD, f32),
            )
            for slot in range(2)
        ],
        compiler_params=PARAMS,
        name="attend",
    )(prompt_ids, dialogue_lens, prompt_lens, arrived, q_base, kv_base, cotangent, shares)
    sums = lax.all_to_all(message, "dp", 0, 0, tiled=True)
    message = pl.pallas_call(
        steer_kernel,
        out_shape=jax.ShapeDtypeStruct((tensor, 1, steering.shape[0]), f32),
        in_specs=[VMEM, VMEM, VMEM],
        out_specs=VMEM,
        compiler_params=PARAMS,
        name="steer",
    )(sums, w_query, w_kv)
    parts = lax.all_to_all(message, "tensor", 0, 0, tiled=True)
    return (query_grad, kv_grad, jnp.sum(parts, axis=(0, 1)))


def solution(mesh):
    placed = (
        P("dp", "tensor"),
        P(None, "dp", "tensor"),
        P("dp", "tensor"),
        P("dp"),
        P("dp", "tensor"),
        P(None, "dp", "tensor"),
        P(None, None, "dp", "tensor"),
        P("dp"),
        P("dp"),
        P(),
    )
    return jax.shard_map(
        shards,
        mesh=mesh,
        in_specs=placed,
        out_specs=(P("dp", "tensor"), P(None, "dp", "tensor"), P("dp")),
        check_vma=False,
    )
```

time: 109 us -> 98.6 us (0.905)
  blocking collectives: 63.5 us -> 59.9 us
  local copies, waits for them, and re-layouts: 2.47 us -> 0.04 us
  starting transfers between devices: 7.4 us -> 5.83 us
  other arithmetic: 1.76 us -> 0.54 us
    pallas_call x1, Pallas kernels: 10.7 us -> 8.16 us  [shards(): pl.pallas_call(attend_kernel, out_shape=(jax.ShapeDtypeStruct(q_base.shap...]
    unnamed x20 -> x14, local copies, waits for them, and re-layouts: 2.47 us -> 0.04 us
    all_to_all x1, blocking collectives: 32.9 us -> 30.8 us  [shards(): shares = lax.all_to_all(message, 'dp', 0, 0, tiled=True)]
    pallas_call x1, Pallas kernels: 0.19 us -> 1.86 us  [shards(): pl.pallas_call(project_kernel, out_shape=jax.ShapeDtypeStruct((dp, 2, hal...]
    all_to_all x1, starting transfers between devices: 7.4 us -> 5.83 us  [shards(): arrived = lax.all_to_all(outgoing, 'dp', 0, 0, tiled=True)]
    all_to_all x1, blocking collectives: 21.7 us -> 20.3 us  [shards(): sums = lax.all_to_all(message, 'dp', 0, 0, tiled=True)]
    convert_element_type x1 -> x0, other arithmetic: 1.22 us -> none  [shards(): ids = shares[:, 0, all_width].astype(jnp.int32)]
where the time goes in v2:
time: 98.6 us; the launch traced here: 98.3 us
  blocking collectives  59.9 us (61%)
  waiting for transfers between devices  18.3 us (19%)
  Pallas kernels  11.7 us (12%)
  starting transfers between devices  5.83 us (6%)
  between operations  2.02 us (2%)
    all_to_all x1, blocking collectives, shards(): shares = lax.all_to_all(message, 'dp', 0, 0, tiled=True)  30.8 us
    all_to_all x1, blocking collectives, shards(): sums = lax.all_to_all(message, 'dp', 0, 0, tiled=True)  20.3 us
    all_to_all x1, waiting for transfers between devices, shards(): arrived = lax.all_to_all(outgoing, 'dp', 0, 0, tiled=True)  18.3 us
    all_to_all x1, blocking collectives, shards(): parts = lax.all_to_all(message, 'tensor', 0, 0, tiled=True)  8.83 us
    pallas_call x1, Pallas kernels, shards(): pl.pallas_call(attend_kernel, out_shape=(jax.ShapeDtypeStruct(q_base.shap...  8.16 us
    all_to_all x1, starting transfers between devices, shards(): arrived = lax.all_to_all(outgoing, 'dp', 0, 0, tiled=True)  5.83 us
  transfers between devices with their start and end apart: 1, of which 1 were waited for; matrix products, arithmetic and copies ran while one was open for 0% of the time, Pallas kernels for 0%

profile of v2, /device:TPU:1, one launch (start us, length us, event | category | flops | bytes accessed | tf_op | source)
XLA Modules:
  0.0 98.3 jit_solution(5459307975862563097)
XLA Ops:
  1.3 1.9 %project.1 = bf16[64,2,768]{2,1,0:T(2,128)(2,1)} custom-call(s32[1]{0:T(128)S(6)} %copy.13.prompt_id.ids, f32[1,128]{1,0:T(1,128)} %bitcast.1, bf16[128,1024]{1,0:T(8,128)(2,1)} %w_query.3, bf16[2,128,128]{2,1,0:T(8,128)(2,1)} %w_kv.3), custom_call_target="tpu_custom_call" | custom-call | tf_op jit(solution)/shard_map/project/pallas_call | solution.py:241
  3.1 0.0 copy-start.3
  3.2 30.8 %all_to_all.20.shares.shifts = bf16[64,2,768]{2,1,0:T(2,128)(2,1)S(1)} all-to-all(bf16[64,2,768]{2,1,0:T(2,128)(2,1)} %project.1), channel_id=1, replica_groups=mesh['dp'=64,'tensor'=8] {'dp'}, dimensions={0} | all-to-all | bytes 393216 | tf_op jit(solution)/shard_map/all_to_all | solution.py:255
  33.9 0.0 copy-done.3
  33.9 0.0 copy-start.5
  33.9 1.4 %pick.1 = bf16[64,2,16,128]{3,2,1,0:T(8,128)(2,1)} custom-call(bf16[64,2,768]{2,1,0:T(2,128)(2,1)S(1)} %all_to_all.20.shares.shifts, bf16[2,32,16,128]{3,2,1,0:T(8,128)(2,1)S(1)} %copy-done.3), custom_call_target="tpu_custom_call" | custom-call | tf_op jit(solution)/shard_map/pick/pallas_call | solution.py:256
  35.4 0.0 copy-start.1
  35.4 0.0 copy-start.2
  35.4 5.8 %all-to-all-start.1 = ((bf16[64,2,16,128]{3,2,1,0:T(8,128)(2,1)}), bf16[64,2,16,128]{3,2,1,0:T(8,128)(2,1)S(1)}, u32[]{:S(2)}, u32[]{:S(2)}) async-start(bf16[64,2,16,128]{3,2,1,0:T(8,128)(2,1)} %pick.1), calls=%async_computation.1 | async-start | bytes 1048576 | tf_op jit(solution)/shard_map/all_to_all | solution.py:269
  41.2 0.0 copy-start.6
  41.9 18.3 %all-to-all-done.1.arrived = bf16[64,2,16,128]{3,2,1,0:T(8,128)(2,1)S(1)} async-done(((bf16[64,2,16,128]{3,2,1,0:T(8,128)(2,1)}), bf16[64,2,16,128]{3,2,1,0:T(8,128)(2,1)S(1)}, u32[]{:S(2)}, u32[]{:S(2)}) %all-to-all-start.1) | async-done | bytes 524320 | tf_op jit(solution)/shard_map/all_to_all | solution.py:269
  60.1 0.0 copy-done.5
  60.1 0.0 copy-done.1
  60.1 0.0 copy-done.2
  60.1 0.0 copy-done.6
  60.2 8.2 %attend.1 = (bf16[256,1024]{1,0:T(8,128)(2,1)}, bf16[2,256,128]{2,1,0:T(8,128)(2,1)}, bf16[64,2,640]{2,1,0:T(2,128)(2,1)S(1)}) custom-call(s32[1]{0:T(128)S(6)} %copy.13.prompt_id.ids, s32[1]{0:T(128)S(6)} %copy.14.lens, s32[32]{0:T(128)S(1)} %copy-done.6, bf16[64,2,16,128]{3,2,1,0:T(8,128)(2,1)S(1)} %all-to-all-done.1.arrived, ...), custom_call_target="tpu_custom_call" | custom-call | tf_op jit(solution)/shard_map/attend/pallas_call | solution.py:271
  68.3 0.0 copy-start
  68.3 0.0 copy-start.4
  68.3 20.3 %all_to_all.21.sums = bf16[64,2,640]{2,1,0:T(2,128)(2,1)S(1)} all-to-all(bf16[64,2,640]{2,1,0:T(2,128)(2,1)S(1)} %get-tuple-element.8), channel_id=1, replica_groups=mesh['dp'=64,'tensor'=8] {'dp'}, dimensions={0} | all-to-all | bytes 327680 | tf_op jit(solution)/shard_map/all_to_all | solution.py:304
  88.6 0.0 copy-done
  88.6 0.0 copy-done.4
  88.6 0.3 steer.1
  88.9 8.8 %all_to_all.22 = f32[8,1,128]{2,1,0:T(1,128)S(1)} all-to-all(f32[8,1,128]{2,1,0:T(1,128)S(1)} %steer.1), channel_id=1, replica_groups=mesh['dp'=64,'tensor'=8] {'tensor'}, dimensions={0} | all-to-all | bytes 8192 | tf_op jit(solution)/shard_map/all_to_all | solution.py:313
  97.7 0.5 reduce_sum.9
Async XLA Ops:
  3.1 30.8 %copy-start.3 = (bf16[2,32,16,128]{3,2,1,0:T(8,128)(2,1)S(1)}, bf16[2,32,16,128]{3,2,1,0:T(8,128)(2,1)}, u32[]{:S(2)}) copy-start(bf16[2,32,16,128]{3,2,1,0:T(8,128)(2,1)} %cache.1) | copy-start | bytes 786436
  33.9 26.2 %copy-start.5 = (bf16[2,256,128]{2,1,0:T(8,128)(2,1)S(1)}, bf16[2,256,128]{2,1,0:T(8,128)(2,1)}, u32[]{:S(2)}) copy-start(bf16[2,256,128]{2,1,0:T(8,128)(2,1)} %kv_ref.1) | copy-start | bytes 393220
  35.4 24.8 %copy-start.1 = (bf16[256,1024]{1,0:T(8,128)(2,1)S(1)}, bf16[256,1024]{1,0:T(8,128)(2,1)}, u32[]{:S(2)}) copy-start(bf16[256,1024]{1,0:T(8,128)(2,1)} %q_ref.1) | copy-start | bytes 1572868
  35.4 24.8 %copy-start.2 = (bf16[256,1024]{1,0:T(8,128)(2,1)S(1)}, bf16[256,1024]{1,0:T(8,128)(2,1)}, u32[]{:S(2)}) copy-start(bf16[256,1024]{1,0:T(8,128)(2,1)} %cot_ref.1) | copy-start | bytes 1572868
  35.4 24.8 %all-to-all-start.1 = ((bf16[64,2,16,128]{3,2,1,0:T(8,128)(2,1)}), bf16[64,2,16,128]{3,2,1,0:T(8,128)(2,1)S(1)}, u32[]{:S(2)}, u32[]{:S(2)}) async-start(bf16[64,2,16,128]{3,2,1,0:T(8,128)(2,1)} %pick.1), calls=%async_computation.1 | async-start | bytes 1048576 | tf_op jit(solution)/shard_map/all_to_all | solution.py:269
  41.2 18.9 %copy-start.6 = (s32[32]{0:T(128)S(1)}, s32[32]{0:T(128)}, u32[]{:S(2)}) copy-start(s32[32]{0:T(128)} %prompt_lens.1) | copy-start | bytes 388
  68.3 20.3 %copy-start = (bf16[128,1024]{1,0:T(8,128)(2,1)S(1)}, bf16[128,1024]{1,0:T(8,128)(2,1)}, u32[]{:S(2)}) copy-start(bf16[128,1024]{1,0:T(8,128)(2,1)} %w_query.3) | copy-start | bytes 786436
  68.3 20.3 %copy-start.4 = (bf16[2,128,128]{2,1,0:T(8,128)(2,1)S(1)}, bf16[2,128,128]{2,1,0:T(8,128)(2,1)}, u32[]{:S(2)}) copy-start(bf16[2,128,128]{2,1,0:T(8,128)(2,1)} %w_kv.3) | copy-start | bytes 196612

commit v3 on v2

--- a/solution.py
+++ b/solution.py
@@ -9,7 +9,8 @@
 from jax.sharding import PartitionSpec as P
 
 HD = 128
-ROWS = 16
+ROWS = 32
+TILE = 256
 MASKED = -1e30
 NN = (((1,), (0,)), ((), ()))
 NT = (((1,), (1,)), ((), ()))
@@ -35,7 +36,7 @@
 def in_halves(chunks):
     half = len(chunks) // 2
     rows = [jnp.concatenate(chunks[:half], axis=1), jnp.concatenate(chunks[half:], axis=1)]
-    return jnp.concatenate(rows, axis=0).astype(jnp.bfloat16)
+    return jnp.concatenate(rows, axis=0)
 
 
 def summed(blocks):
@@ -57,27 +58,41 @@
     ]
     for copy in copies:
         copy.start()
-    mark = jnp.full((1, HD), prompt_id[0], jnp.int32).astype(jnp.float32)
+    mark = jnp.full((1, HD), prompt_id[0], jnp.int32)
     for copy in copies:
         copy.wait()
     thirds = in_thirds(vector[...])
     parts = [jnp.sum(dot(thirds, w[...], NN), 0, keepdims=True) for w in (wq, wkv.at[0], wkv.at[1])]
     row = jnp.concatenate(parts, axis=1)
-    chunks = [row[:, at : at + HD] for at in range(0, row.shape[1], HD)]
+    peak = jnp.max(jnp.abs(row), 1, keepdims=True)
+    power = jnp.clip(jnp.floor(14.9 - jnp.log2(peak)), -60.0, 60.0)
+    whole = jnp.floor(row * jnp.exp2(power) + 0.5).astype(jnp.int32)
+    scale = jnp.broadcast_to(power, (1, HD)).astype(jnp.int32)
+    chunks = [whole[:, at : at + HD] for at in range(0, whole.shape[1], HD)]
     half = len(chunks) // 2
-    block = in_halves(chunks[:half] + [mark] + chunks[half:] + [mark])
+    block = in_halves(chunks[:half] + [mark] + chunks[half:] + [scale]).astype(jnp.int16)
     for peer in range(message.shape[0]):
         message[peer] = block
+
+
+def shifts_from(shares):
+    last = shares.shape[2] - HD
+    total = jnp.zeros((2, last), jnp.float32)
+    for peer in range(shares.shape[0]):
+        block = shares[peer].astype(jnp.int32).astype(jnp.float32)
+        scale = jnp.exp2(-block[1:, last:])
+        total = total + block[:, :last] * jnp.concatenate([scale] * (last // HD), axis=1)
+    return total
 
 
 def pick_kernel(shares, cache, outgoing, marks, ids, sems):
     peers = shares.shape[0]
     last = shares.shape[2] - HD
     lane = lax.broadcasted_iota(jnp.int32, (2, HD), 1)
-    found = jnp.zeros((2, HD), jnp.float32)
+    found = jnp.zeros((2, HD), jnp.int32)
     for peer in range(peers):
-        found = jnp.where(lane == peer, shares[peer, :, last:].astype(jnp.float32), found)
-    marks[...] = found[:1].astype(jnp.int32)
+        found = jnp.where(lane == peer, shares[peer, :, last:].astype(jnp.int32), found)
+    marks[...] = found[:1]
     copy = pltpu.make_async_copy(marks, ids, sems.at[0])
     copy.start()
     copy.wait()
@@ -112,12 +127,10 @@
     grads1,
     weights0,
     weights1,
-    queries0,
-    queries1,
-    outs0,
-    outs1,
     factors0,
     factors1,
+    queries,
+    outs,
 ):
     f32, bf16 = jnp.float32, jnp.bfloat16
     span = arrived.shape[0] * arrived.shape[2]
@@ -127,8 +140,8 @@
     to_log2 = scale * math.log2(math.e)
     live = lens[0]
     prompt_live = prompt_lens[ids[0]]
-    total = summed(shifts)
-    shift = [chunk_of(total[:, : total.shape[1] - HD], c, heads + 2) for c in range(heads + 2)]
+    total = shifts_from(shifts)
+    shift = [chunk_of(total, chunk, heads + 2) for chunk in range(heads + 2)]
     pre_keys = arrived[:, 0].reshape(span, HD)
     pre_values = arrived[:, 1].reshape(span, HD)
     own_keys = (kv_ref[0].astype(f32) + shift[heads]).astype(bf16)
@@ -152,57 +165,80 @@
     lane = lax.broadcasted_iota(jnp.int32, (own, HD), 1)
     scores, slopes = (scores0, scores1), (slopes0, slopes1)
     grads, weights = (grads0, grads1), (weights0, weights1)
-    queries, outs, factors = (queries0, queries1), (outs0, outs1), (factors0, factors1)
+    factors = (factors0, factors1)
     sums = []
-
-    def products(head):
-        slot, columns = head % 2, slice(head * HD, (head + 1) * HD)
+    tiles = (span + own) // TILE
+
+    def operands(head):
+        columns = slice(head * HD, (head + 1) * HD)
         query = (q_ref[:, columns].astype(f32) + shift[head]).astype(bf16)
         grad = jnp.where(token < live, cot_ref[:, columns].astype(f32), 0.0).astype(bf16)
-        queries[slot][...] = query
-        outs[slot][...] = grad
+        queries[:, columns] = query
+        outs[:, columns] = grad
         scaled = query.astype(f32) * to_log2
         high = scaled.astype(bf16)
         low = jnp.where(lane == HD - 1, 1.0, scaled - high.astype(f32)).astype(bf16)
-        scores[slot][...] = dot(jnp.concatenate([high, low], axis=1), keys_t[...], NN)
-        slopes[slot][...] = dot(grad, values_t[...], NN)
-
-    def softmax(head):
-        slot = head % 2
-        for at in range(0, own, ROWS):
-            rows = slice(at, at + ROWS)
-            score = scores[slot][rows]
-            score = jnp.concatenate([score[:, :span], score[:, span:] + causal[rows]], axis=1)
-            prob = jnp.exp2(score - jnp.max(score, 1, keepdims=True))
-            slope = slopes[slot][rows]
-            inverse = 1.0 / jnp.sum(prob, 1, keepdims=True)
-            delta = jnp.sum(prob * slope, 1, keepdims=True) * inverse
-            grads[slot][rows] = (prob * (slope - delta)).astype(bf16)
-            weights[slot][rows] = (prob[:, span:] * inverse).astype(bf16)
-            factors[slot][rows] = jnp.broadcast_to(inverse * scale, (ROWS, HD))
-
-    def gradients(head):
+        return jnp.concatenate([high, low], axis=1), grad
+
+    def product(head, at, query, grad):
+        slot, part = head % 2, slice(at % tiles * TILE, (at % tiles + 1) * TILE)
+        if at < tiles:
+            scores[slot][:, part] = dot(query, keys_t[:, part], NN)
+        else:
+            slopes[slot][:, part] = dot(grad, values_t[:, part], NN)
+
+    def softmax(head, at):
+        slot, rows = head % 2, slice(at * ROWS, (at + 1) * ROWS)
+        score = scores[slot][rows]
+        score = jnp.concatenate([score[:, :span], score[:, span:] + causal[rows]], axis=1)
+        prob = jnp.exp2(score - jnp.max(score, 1, keepdims=True))
+        slope = slopes[slot][rows]
+        inverse = 1.0 / jnp.sum(prob, 1, keepdims=True)
+        delta = jnp.sum(prob * slope, 1, keepdims=True) * inverse
+        grads[slot][rows] = (prob * (slope - delta)).astype(bf16)
+        weights[slot][rows] = (prob[:, span:] * inverse).astype(bf16)
+        factors[slot][rows] = jnp.broadcast_to(inverse * scale, (ROWS, HD))
+
+    def gradient(head, at, total):
         slot, columns = head % 2, slice(head * HD, (head + 1) * HD)
-        factor = factors[slot][...]
-        grad_query = dot(grads[slot][...], keys[...], NN) * factor
-        dq_ref[:, columns] = grad_query.astype(bf16)
-        sums.append(jnp.sum(grad_query, 0, keepdims=True))
-        query = (queries[slot][...].astype(f32) * factor).astype(bf16)
-        grad_keys[...] += dot(grads[slot][:, span:], query, TN)
-        grad_values[...] += dot(weights[slot][...], outs[slot][...], TN)
-
-    products(0)
+        if at < tiles:
+            part = slice(at * TILE, (at + 1) * TILE)
+            term = dot(grads[slot][:, part], keys[part], NN)
+            return term if total is None else total + term
+        if at == tiles:
+            factor = factors[slot][...]
+            total = total * factor
+            dq_ref[:, columns] = total.astype(bf16)
+            sums.append(jnp.sum(total, 0, keepdims=True))
+            query = (queries[:, columns].astype(f32) * factor).astype(bf16)
+            grad_keys[...] += dot(grads[slot][:, span:], query, TN)
+        else:
+            grad_values[...] += dot(weights[slot][...], outs[:, columns], TN)
+        return total
+
+    current = operands(0)
+    for at in range(2 * tiles):
+        product(0, at, *current)
+    chunks = own // ROWS
     for head in range(heads):
-        if head > 0:
-            gradients(head - 1)
         if head + 1 < heads:
-            products(head + 1)
-        softmax(head)
-    gradients(heads - 1)
+            current = operands(head + 1)
+        total, done, made = None, 0, 0
+        for chunk in range(chunks):
+            while head + 1 < heads and made < 2 * tiles * (chunk + 1) // chunks:
+                product(head + 1, made, *current)
+                made += 1
+            while head > 0 and done < (tiles + 2) * (chunk + 1) // chunks:
+                total = gradient(head - 1, done, total)
+                done += 1
+            softmax(head, chunk)
+    total = None
+    for at in range(tiles + 2):
+        total = gradient(heads - 1, at, total)
     dkv_ref[0] = grad_keys[...].astype(bf16)
     dkv_ref[1] = grad_values[...].astype(bf16)
     last = [jnp.sum(grad_keys[...], 0, keepdims=True), jnp.sum(grad_values[...], 0, keepdims=True)]
-    block = in_halves(sums + last)
+    block = in_halves(sums + last).astype(bf16)
     for peer in range(message.shape[0]):
         message[peer] = block
 
@@ -240,7 +276,7 @@
     bf16 = jnp.bfloat16
     message = pl.pallas_call(
         project_kernel,
-        out_shape=jax.ShapeDtypeStruct((dp, 2, half_width + HD), bf16),
+        out_shape=jax.ShapeDtypeStruct((dp, 2, half_width + HD), jnp.int16),
         in_specs=[SMEM, HBM, HBM, HBM],
         out_specs=VMEM,
         scratch_shapes=[
@@ -292,12 +328,11 @@
                 (keys_held, f32),
                 (keys_held, bf16),
                 (tokens, bf16),
-                (HD, bf16),
-                (HD, bf16),
                 (HD, f32),
             )
             for slot in range(2)
-        ],
+        ]
+        + [pltpu.VMEM(q_base.shape, bf16), pltpu.VMEM(q_base.shape, bf16)],
         compiler_params=PARAMS,
         name="attend",
     )(prompt_ids, dialogue_lens, prompt_lens, arrived, q_base, kv_base, cotangent, shares)

time: 98.6 us -> 98.4 us (level)
  no operation moved by 1% of the time
where the time goes in v3:
time: 98.4 us; the launch traced here: 98 us
  blocking collectives  59.9 us (61%)
  waiting for transfers between devices  18.3 us (19%)
  Pallas kernels  11.5 us (12%)
  starting transfers between devices  5.83 us (6%)
  between operations  2.02 us (2%)
    all_to_all x1, blocking collectives, shards(): shares = lax.all_to_all(message, 'dp', 0, 0, tiled=True)  30.8 us
    all_to_all x1, blocking collectives, shards(): sums = lax.all_to_all(message, 'dp', 0, 0, tiled=True)  20.3 us
    all_to_all x1, waiting for transfers between devices, shards(): arrived = lax.all_to_all(outgoing, 'dp', 0, 0, tiled=True)  18.3 us
    all_to_all x1, blocking collectives, shards(): parts = lax.all_to_all(message, 'tensor', 0, 0, tiled=True)  8.84 us
    pallas_call x1, Pallas kernels, shards(): pl.pallas_call(attend_kernel, out_shape=(jax.ShapeDtypeStruct(q_base.shap...  7.83 us
    all_to_all x1, starting transfers between devices, shards(): arrived = lax.all_to_all(outgoing, 'dp', 0, 0, tiled=True)  5.83 us
  transfers between devices with their start and end apart: 1, of which 1 were waited for; matrix products, arithmetic and copies ran while one was open for 0% of the time, Pallas kernels for 0%

profile of v3, /device:TPU:1, one launch (start us, length us, event | category | flops | bytes accessed | tf_op | source)
XLA Modules:
  0.0 98.0 jit_solution(8312489633923075986)
XLA Ops:
  1.3 2.0 %project.1 = s16[64,2,768]{2,1,0:T(2,128)(2,1)} custom-call(s32[1]{0:T(128)S(6)} %copy.13.prompt_id.ids, f32[1,128]{1,0:T(1,128)} %bitcast.1, bf16[128,1024]{1,0:T(8,128)(2,1)} %w_query.3, bf16[2,128,128]{2,1,0:T(8,128)(2,1)} %w_kv.3), custom_call_target="tpu_custom_call" | custom-call | tf_op jit(solution)/shard_map/project/pallas_call | solution.py:277
  3.2 0.0 copy-start.3
  3.3 30.8 %all_to_all.20.shares.shifts = s16[64,2,768]{2,1,0:T(2,128)(2,1)S(1)} all-to-all(s16[64,2,768]{2,1,0:T(2,128)(2,1)} %project.1), channel_id=1, replica_groups=mesh['dp'=64,'tensor'=8] {'dp'}, dimensions={0} | all-to-all | bytes 393216 | tf_op jit(solution)/shard_map/all_to_all | solution.py:291
  34.0 0.0 copy-done.3
  34.0 0.0 copy-start.5
  34.0 1.4 %pick.1 = bf16[64,2,16,128]{3,2,1,0:T(8,128)(2,1)} custom-call(s16[64,2,768]{2,1,0:T(2,128)(2,1)S(1)} %all_to_all.20.shares.shifts, bf16[2,32,16,128]{3,2,1,0:T(8,128)(2,1)S(1)} %copy-done.3), custom_call_target="tpu_custom_call" | custom-call | tf_op jit(solution)/shard_map/pick/pallas_call | solution.py:292
  35.4 0.0 copy-start.1
  35.5 0.0 copy-start.2
  35.5 5.8 %all-to-all-start.1 = ((bf16[64,2,16,128]{3,2,1,0:T(8,128)(2,1)}), bf16[64,2,16,128]{3,2,1,0:T(8,128)(2,1)S(1)}, u32[]{:S(2)}, u32[]{:S(2)}) async-start(bf16[64,2,16,128]{3,2,1,0:T(8,128)(2,1)} %pick.1), calls=%async_computation.1 | async-start | bytes 1048576 | tf_op jit(solution)/shard_map/all_to_all | solution.py:305
  41.3 0.0 copy-start.6
  42.0 18.3 %all-to-all-done.1.arrived = bf16[64,2,16,128]{3,2,1,0:T(8,128)(2,1)S(1)} async-done(((bf16[64,2,16,128]{3,2,1,0:T(8,128)(2,1)}), bf16[64,2,16,128]{3,2,1,0:T(8,128)(2,1)S(1)}, u32[]{:S(2)}, u32[]{:S(2)}) %all-to-all-start.1) | async-done | bytes 524320 | tf_op jit(solution)/shard_map/all_to_all | solution.py:305
  60.2 0.0 copy-done.5
  60.2 0.0 copy-done.1
  60.2 0.0 copy-done.2
  60.2 0.0 copy-done.6
  60.3 7.8 %attend.1 = (bf16[256,1024]{1,0:T(8,128)(2,1)}, bf16[2,256,128]{2,1,0:T(8,128)(2,1)}, bf16[64,2,640]{2,1,0:T(2,128)(2,1)S(1)}) custom-call(s32[1]{0:T(128)S(6)} %copy.13.prompt_id.ids, s32[1]{0:T(128)S(6)} %copy.14.lens, s32[32]{0:T(128)S(1)} %copy-done.6, bf16[64,2,16,128]{3,2,1,0:T(8,128)(2,1)S(1)} %all-to-all-done.1.arrived, ...), custom_call_target="tpu_custom_call" | custom-call | tf_op jit(solution)/shard_map/attend/pallas_call | solution.py:307
  68.1 0.0 copy-start
  68.1 0.0 copy-start.4
  68.1 20.3 %all_to_all.21.sums = bf16[64,2,640]{2,1,0:T(2,128)(2,1)S(1)} all-to-all(bf16[64,2,640]{2,1,0:T(2,128)(2,1)S(1)} %get-tuple-element.8), channel_id=1, replica_groups=mesh['dp'=64,'tensor'=8] {'dp'}, dimensions={0} | all-to-all | bytes 327680 | tf_op jit(solution)/shard_map/all_to_all | solution.py:339
  88.4 0.0 copy-done
  88.4 0.0 copy-done.4
  88.4 0.3 steer.1
  88.7 8.8 %all_to_all.22 = f32[8,1,128]{2,1,0:T(1,128)S(1)} all-to-all(f32[8,1,128]{2,1,0:T(1,128)S(1)} %steer.1), channel_id=1, replica_groups=mesh['dp'=64,'tensor'=8] {'tensor'}, dimensions={0} | all-to-all | bytes 8192 | tf_op jit(solution)/shard_map/all_to_all | solution.py:348
  97.5 0.5 reduce_sum.9
Async XLA Ops:
  3.2 30.8 %copy-start.3 = (bf16[2,32,16,128]{3,2,1,0:T(8,128)(2,1)S(1)}, bf16[2,32,16,128]{3,2,1,0:T(8,128)(2,1)}, u32[]{:S(2)}) copy-start(bf16[2,32,16,128]{3,2,1,0:T(8,128)(2,1)} %cache.1) | copy-start | bytes 786436
  34.0 26.2 %copy-start.5 = (bf16[2,256,128]{2,1,0:T(8,128)(2,1)S(1)}, bf16[2,256,128]{2,1,0:T(8,128)(2,1)}, u32[]{:S(2)}) copy-start(bf16[2,256,128]{2,1,0:T(8,128)(2,1)} %kv_ref.1) | copy-start | bytes 393220
  35.4 24.8 %copy-start.1 = (bf16[256,1024]{1,0:T(8,128)(2,1)S(1)}, bf16[256,1024]{1,0:T(8,128)(2,1)}, u32[]{:S(2)}) copy-start(bf16[256,1024]{1,0:T(8,128)(2,1)} %q_ref.1) | copy-start | bytes 1572868
  35.5 24.8 %copy-start.2 = (bf16[256,1024]{1,0:T(8,128)(2,1)S(1)}, bf16[256,1024]{1,0:T(8,128)(2,1)}, u32[]{:S(2)}) copy-start(bf16[256,1024]{1,0:T(8,128)(2,1)} %cot_ref.1) | copy-start | bytes 1572868
  35.5 24.8 %all-to-all-start.1 = ((bf16[64,2,16,128]{3,2,1,0:T(8,128)(2,1)}), bf16[64,2,16,128]{3,2,1,0:T(8,128)(2,1)S(1)}, u32[]{:S(2)}, u32[]{:S(2)}) async-start(bf16[64,2,16,128]{3,2,1,0:T(8,128)(2,1)} %pick.1), calls=%async_computation.1 | async-start | bytes 1048576 | tf_op jit(solution)/shard_map/all_to_all | solution.py:305
  41.3 18.9 %copy-start.6 = (s32[32]{0:T(128)S(1)}, s32[32]{0:T(128)}, u32[]{:S(2)}) copy-start(s32[32]{0:T(128)} %prompt_lens.1) | copy-start | bytes 388
  68.1 20.3 %copy-start = (bf16[128,1024]{1,0:T(8,128)(2,1)S(1)}, bf16[128,1024]{1,0:T(8,128)(2,1)}, u32[]{:S(2)}) copy-start(bf16[128,1024]{1,0:T(8,128)(2,1)} %w_query.3) | copy-start | bytes 786436
  68.1 20.3 %copy-start.4 = (bf16[2,128,128]{2,1,0:T(8,128)(2,1)S(1)}, bf16[2,128,128]{2,1,0:T(8,128)(2,1)}, u32[]{:S(2)}) copy-start(bf16[2,128,128]{2,1,0:T(8,128)(2,1)} %w_kv.3) | copy-start | bytes 196612

commit v4 on v3

--- a/solution.py
+++ b/solution.py
@@ -101,149 +101,200 @@
     pltpu.make_async_copy(outgoing, outgoing, sems.at[1]).wait()
 
 
+def two_parts(query):
+    scaled = query.astype(jnp.float32) * (math.log2(math.e) / math.sqrt(HD))
+    high = scaled.astype(jnp.bfloat16)
+    lane = lax.broadcasted_iota(jnp.int32, query.shape, 1)
+    low = jnp.where(lane == HD - 1, 1.0, scaled - high.astype(jnp.float32)).astype(jnp.bfloat16)
+    return jnp.concatenate([high, low], axis=1)
+
+
+def column(block, at):
+    lane = lax.broadcasted_iota(jnp.int32, block.shape, 1)
+    return jnp.sum(jnp.where(lane == at, block, 0.0), 1, keepdims=True)
+
+
+def fill_own(live, keys, keys_two, causal):
+    lane = lax.broadcasted_iota(jnp.int32, keys.shape, 1)
+    keys_two[:, :HD] = keys
+    keys_two[:, HD:] = jnp.where(lane == HD - 1, 0.0, keys.astype(jnp.float32)).astype(jnp.bfloat16)
+    token_at = lax.broadcasted_iota(jnp.int32, causal.shape, 0)
+    key_at = lax.broadcasted_iota(jnp.int32, causal.shape, 1)
+    causal[...] = jnp.where((key_at <= token_at) & (key_at < live), 0.0, MASKED)
+
+
+def shift_kernel(lens, shares, q_ref, kv_ref, cot_ref, outgoing, queries, outs, own):
+    del outgoing
+    f32, bf16 = jnp.float32, jnp.bfloat16
+    heads = q_ref.shape[1] // HD
+    total = shifts_from(shares)
+    shift = [chunk_of(total, chunk, heads + 2) for chunk in range(heads + 2)]
+    for c in range(2):
+        own[c] = (kv_ref[c].astype(f32) + shift[heads + c]).astype(bf16)
+    token = lax.broadcasted_iota(jnp.int32, (q_ref.shape[0], HD), 0)
+    for head in range(heads):
+        columns = slice(head * HD, (head + 1) * HD)
+        queries[:, columns] = (q_ref[:, columns].astype(f32) + shift[head]).astype(bf16)
+        grad = jnp.where(token < lens[0], cot_ref[:, columns].astype(f32), 0.0)
+        outs[:, columns] = grad.astype(bf16)
+
+
+def prepare_kernel(
+    ids, prompt_lens, lens, queries, outs, own, stats, sloped, plain, keys_two, causal
+):
+    f32, bf16 = jnp.float32, jnp.bfloat16
+    heads = queries.shape[1] // HD
+    fill_own(lens[0], own[0], keys_two, causal)
+    prompt_live = jnp.full((queries.shape[0], 1), prompt_lens[ids[0]], jnp.int32)
+    stats[:, 3 * heads : 3 * heads + 1] = prompt_live.astype(f32)
+    for head in range(heads):
+        columns = slice(head * HD, (head + 1) * HD)
+        score = dot(two_parts(queries[:, columns]), keys_two[...], NT) + causal[...]
+        top = jnp.max(score, 1, keepdims=True)
+        prob = jnp.exp2(score - top)
+        slope = prob * dot(outs[:, columns], own[1], NT)
+        stats[:, head : head + 1] = top
+        stats[:, heads + head : heads + head + 1] = jnp.sum(prob, 1, keepdims=True)
+        stats[:, 2 * heads + head : 2 * heads + head + 1] = jnp.sum(slope, 1, keepdims=True)
+        sloped[head] = dot(slope.astype(bf16), own[0], NN).astype(bf16)
+        plain[head] = dot(prob.astype(bf16), own[0], NN).astype(bf16)
+
+
 def attend_kernel(
-    ids,
-    lens,
-    prompt_lens,
     arrived,
-    q_ref,
-    kv_ref,
-    cot_ref,
-    shifts,
+    queries,
+    outs,
+    stats,
+    sloped,
+    plain,
     dq_ref,
-    dkv_ref,
     message,
+    final,
     keys,
     keys_t,
     values_t,
-    grad_keys,
-    grad_values,
-    causal,
     scores0,
     scores1,
     slopes0,
     slopes1,
     grads0,
     grads1,
-    weights0,
-    weights1,
     factors0,
     factors1,
-    queries,
-    outs,
+    terms0,
+    terms1,
 ):
     f32, bf16 = jnp.float32, jnp.bfloat16
     span = arrived.shape[0] * arrived.shape[2]
-    own = kv_ref.shape[1]
-    heads = q_ref.shape[1] // HD
+    tokens = queries.shape[0]
+    heads = queries.shape[1] // HD
     scale = 1.0 / math.sqrt(HD)
-    to_log2 = scale * math.log2(math.e)
-    live = lens[0]
-    prompt_live = prompt_lens[ids[0]]
-    total = shifts_from(shifts)
-    shift = [chunk_of(total, chunk, heads + 2) for chunk in range(heads + 2)]
-    pre_keys = arrived[:, 0].reshape(span, HD)
-    pre_values = arrived[:, 1].reshape(span, HD)
-    own_keys = (kv_ref[0].astype(f32) + shift[heads]).astype(bf16)
-    own_values = (kv_ref[1].astype(f32) + shift[heads + 1]).astype(bf16)
-    keys[:span] = pre_keys
-    keys[span:] = own_keys
-    keys_t[:HD, :span] = pre_keys.T
-    keys_t[:HD, span:] = own_keys.T
-    values_t[:, :span] = pre_values.T
-    values_t[:, span:] = own_values.T
-    feature = lax.broadcasted_iota(jnp.int32, (HD, span + own), 0)
-    place = lax.broadcasted_iota(jnp.int32, (HD, span + own), 1)
-    barred = jnp.where((place >= prompt_live) & (place < span), MASKED, 0.0)
+    keys[...] = arrived[:, 0].reshape(span, HD)
+    keys_t[:HD] = arrived[:, 0].reshape(span, HD).T
+    values_t[...] = arrived[:, 1].reshape(span, HD).T
+    feature = lax.broadcasted_iota(jnp.int32, (HD, span), 0)
+    prompt_live = jnp.broadcast_to(column(stats[:8], 3 * heads), (8, HD))[:1]
+    prompt_live = jnp.concatenate([prompt_live] * (span // HD), axis=1)
+    place = lax.broadcasted_iota(jnp.int32, (1, span), 1).astype(f32)
+    barred = jnp.where(place >= prompt_live, MASKED, 0.0)
     keys_t[HD:] = jnp.where(feature == HD - 1, barred, keys_t[:HD].astype(f32)).astype(bf16)
-    token_at = lax.broadcasted_iota(jnp.int32, (own, own), 0)
-    key_at = lax.broadcasted_iota(jnp.int32, (own, own), 1)
-    causal[...] = jnp.where((key_at <= token_at) & (key_at < live), 0.0, MASKED)
-    grad_keys[...] = jnp.zeros_like(grad_keys)
-    grad_values[...] = jnp.zeros_like(grad_values)
-    token = lax.broadcasted_iota(jnp.int32, (own, HD), 0)
-    lane = lax.broadcasted_iota(jnp.int32, (own, HD), 1)
     scores, slopes = (scores0, scores1), (slopes0, slopes1)
-    grads, weights = (grads0, grads1), (weights0, weights1)
-    factors = (factors0, factors1)
-    sums = []
-    tiles = (span + own) // TILE
-
-    def operands(head):
-        columns = slice(head * HD, (head + 1) * HD)
-        query = (q_ref[:, columns].astype(f32) + shift[head]).astype(bf16)
-        grad = jnp.where(token < live, cot_ref[:, columns].astype(f32), 0.0).astype(bf16)
-        queries[:, columns] = query
-        outs[:, columns] = grad
-        scaled = query.astype(f32) * to_log2
-        high = scaled.astype(bf16)
-        low = jnp.where(lane == HD - 1, 1.0, scaled - high.astype(f32)).astype(bf16)
-        return jnp.concatenate([high, low], axis=1), grad
-
-    def product(head, at, query, grad):
+    grads, factors, terms = (grads0, grads1), (factors0, factors1), (terms0, terms1)
+    query_sums, key_sums, value_sums = [], [], []
+    tiles = span // TILE
+
+    def columns(head):
+        return slice(head * HD, (head + 1) * HD)
+
+    def product(head, at, query):
         slot, part = head % 2, slice(at % tiles * TILE, (at % tiles + 1) * TILE)
         if at < tiles:
             scores[slot][:, part] = dot(query, keys_t[:, part], NN)
         else:
-            slopes[slot][:, part] = dot(grad, values_t[:, part], NN)
+            slopes[slot][:, part] = dot(outs[:, columns(head)], values_t[:, part], NN)
 
     def softmax(head, at):
         slot, rows = head % 2, slice(at * ROWS, (at + 1) * ROWS)
+        own_top, own_mass, own_slope = (column(stats[rows], n * heads + head) for n in range(3))
         score = scores[slot][rows]
-        score = jnp.concatenate([score[:, :span], score[:, span:] + causal[rows]], axis=1)
-        prob = jnp.exp2(score - jnp.max(score, 1, keepdims=True))
+        top = jnp.maximum(jnp.max(score, 1, keepdims=True), own_top)
+        prob = jnp.exp2(score - top)
+        share = jnp.exp2(own_top - top)
         slope = slopes[slot][rows]
-        inverse = 1.0 / jnp.sum(prob, 1, keepdims=True)
-        delta = jnp.sum(prob * slope, 1, keepdims=True) * inverse
+        inverse = 1.0 / (jnp.sum(prob, 1, keepdims=True) + own_mass * share)
+        delta = (jnp.sum(prob * slope, 1, keepdims=True) + own_slope * share) * inverse
         grads[slot][rows] = (prob * (slope - delta)).astype(bf16)
-        weights[slot][rows] = (prob[:, span:] * inverse).astype(bf16)
-        factors[slot][rows] = jnp.broadcast_to(inverse * scale, (ROWS, HD))
+        factor = inverse * scale
+        factors[slot][rows] = jnp.broadcast_to(factor, (ROWS, HD))
+        own_factor = factor * share
+        term = sloped[head, rows].astype(f32) - delta * plain[head, rows].astype(f32)
+        terms[slot][rows] = term * own_factor
+        by_query = (own_slope - delta * own_mass) * own_factor
+        by_out = own_mass * share * inverse
+        key_sums.append(by_query * queries[rows, columns(head)].astype(f32))
+        value_sums.append(by_out * outs[rows, columns(head)].astype(f32))
+        for n, value in enumerate((top, inverse, delta)):
+            final[rows, n * heads + head : n * heads + head + 1] = value
 
     def gradient(head, at, total):
-        slot, columns = head % 2, slice(head * HD, (head + 1) * HD)
+        slot = head % 2
         if at < tiles:
             part = slice(at * TILE, (at + 1) * TILE)
             term = dot(grads[slot][:, part], keys[part], NN)
             return term if total is None else total + term
-        if at == tiles:
-            factor = factors[slot][...]
-            total = total * factor
-            dq_ref[:, columns] = total.astype(bf16)
-            sums.append(jnp.sum(total, 0, keepdims=True))
-            query = (queries[:, columns].astype(f32) * factor).astype(bf16)
-            grad_keys[...] += dot(grads[slot][:, span:], query, TN)
-        else:
-            grad_values[...] += dot(weights[slot][...], outs[:, columns], TN)
+        total = total * factors[slot][...] + terms[slot][...]
+        dq_ref[:, columns(head)] = total.astype(bf16)
+        query_sums.append(jnp.sum(total, 0, keepdims=True))
         return total
 
-    current = operands(0)
+    query = two_parts(queries[:, columns(0)])
     for at in range(2 * tiles):
-        product(0, at, *current)
-    chunks = own // ROWS
+        product(0, at, query)
+    chunks = tokens // ROWS
     for head in range(heads):
         if head + 1 < heads:
-            current = operands(head + 1)
+            query = two_parts(queries[:, columns(head + 1)])
         total, done, made = None, 0, 0
         for chunk in range(chunks):
             while head + 1 < heads and made < 2 * tiles * (chunk + 1) // chunks:
-                product(head + 1, made, *current)
+                product(head + 1, made, query)
                 made += 1
-            while head > 0 and done < (tiles + 2) * (chunk + 1) // chunks:
+            while head > 0 and done < (tiles + 1) * (chunk + 1) // chunks:
                 total = gradient(head - 1, done, total)
                 done += 1
             softmax(head, chunk)
     total = None
-    for at in range(tiles + 2):
+    for at in range(tiles + 1):
         total = gradient(heads - 1, at, total)
-    dkv_ref[0] = grad_keys[...].astype(bf16)
-    dkv_ref[1] = grad_values[...].astype(bf16)
-    last = [jnp.sum(grad_keys[...], 0, keepdims=True), jnp.sum(grad_values[...], 0, keepdims=True)]
-    block = in_halves(sums + last).astype(bf16)
+    last = [jnp.sum(sum(rows), 0, keepdims=True) for rows in (key_sums, value_sums)]
+    block = in_halves(query_sums + last).astype(bf16)
     for peer in range(message.shape[0]):
         message[peer] = block
 
 
-def steer_kernel(sums, w_query, w_kv, message):
+def finish_kernel(lens, queries, outs, own, final, dkv_ref, token, keys_two, causal):
+    bf16 = jnp.bfloat16
+    heads = queries.shape[1] // HD
+    fill_own(lens[0], own[0], keys_two, causal)
+    grad_keys = grad_values = None
+    for head in range(heads):
+        columns = slice(head * HD, (head + 1) * HD)
+        top, inverse, delta = (column(final[...], n * heads + head) for n in range(3))
+        query, grad = queries[:, columns], outs[:, columns]
+        score = dot(two_parts(query), keys_two[...], NT) + causal[...]
+        prob = jnp.exp2(score - top) * inverse
+        mine = (prob * (dot(grad, own[1], NT) - delta) * (1.0 / math.sqrt(HD))).astype(bf16)
+        by_key = dot(mine, query, TN)
+        by_value = dot(prob.astype(bf16), grad, TN)
+        grad_keys = by_key if head == 0 else grad_keys + by_key
+        grad_values = by_value if head == 0 else grad_values + by_value
+    dkv_ref[0] = grad_keys.astype(bf16)
+    dkv_ref[1] = grad_values.astype(bf16)
+    token[...] = jnp.zeros_like(token)
+
+
+def steer_kernel(sums, w_query, w_kv, token, message):
+    del token
     total = summed(sums)
     heads = w_query.shape[1] // HD
     chunks = [chunk_of(total, chunk, heads + 2) for chunk in range(heads + 2)]
@@ -303,48 +354,75 @@
         name="pick",
     )(shares, prompt_cache)
     arrived = lax.all_to_all(outgoing, "dp", 0, 0, tiled=True)
-    keys_held = dp * positions + tokens
-    query_grad, kv_grad, message = pl.pallas_call(
+    heads = width // HD
+    span = dp * positions
+    by_head = jax.ShapeDtypeStruct((heads, tokens, HD), bf16)
+    by_row = jax.ShapeDtypeStruct((tokens, HD), f32)
+    own_scratch = [pltpu.VMEM((tokens, 2 * HD), bf16), pltpu.VMEM((tokens, tokens), f32)]
+    queries, outs, own = pl.pallas_call(
+        shift_kernel,
+        out_shape=(
+            jax.ShapeDtypeStruct((tokens, width), bf16),
+            jax.ShapeDtypeStruct((tokens, width), bf16),
+            jax.ShapeDtypeStruct((2, tokens, HD), bf16),
+        ),
+        in_specs=[SMEM, VMEM, VMEM, VMEM, VMEM, HBM],
+        out_specs=(VMEM,) * 3,
+        compiler_params=PARAMS,
+        name="shift",
+    )(dialogue_lens, shares, q_base, kv_base, cotangent, outgoing)
+    stats, sloped, plain = pl.pallas_call(
+        prepare_kernel,
+        out_shape=(by_row, by_head, by_head),
+        in_specs=[SMEM, SMEM, SMEM, VMEM, VMEM, VMEM],
+        out_specs=(VMEM,) * 3,
+        scratch_shapes=own_scratch,
+        compiler_params=PARAMS,
+        name="prepare",
+    )(prompt_ids, prompt_lens, dialogue_lens, queries, outs, own)
+    query_grad, message, final = pl.pallas_call(
         attend_kernel,
         out_shape=(
-            jax.ShapeDtypeStruct(q_base.shape, jnp.bfloat16),
-            jax.ShapeDtypeStruct(kv_base.shape, jnp.bfloat16),
+            jax.ShapeDtypeStruct(q_base.shape, bf16),
             jax.ShapeDtypeStruct((dp, 2, half_width), bf16),
+            by_row,
         ),
-        in_specs=[SMEM, SMEM, SMEM, VMEM, VMEM, VMEM, VMEM, VMEM],
+        in_specs=[VMEM] * 6,
         out_specs=(VMEM, VMEM, VMEM),
         scratch_shapes=[
-            pltpu.VMEM((keys_held, HD), bf16),
-            pltpu.VMEM((2 * HD, keys_held), bf16),
-            pltpu.VMEM((HD, keys_held), bf16),
-            pltpu.VMEM((tokens, HD), f32),
-            pltpu.VMEM((tokens, HD), f32),
-            pltpu.VMEM((tokens, tokens), f32),
+            pltpu.VMEM((span, HD), bf16),
+            pltpu.VMEM((2 * HD, span), bf16),
+            pltpu.VMEM((HD, span), bf16),
         ]
         + [
             pltpu.VMEM((tokens, columns), kind)
-            for columns, kind in (
-                (keys_held, f32),
-                (keys_held, f32),
-                (keys_held, bf16),
-                (tokens, bf16),
-                (HD, f32),
-            )
+            for columns, kind in ((span, f32), (span, f32), (span, bf16), (HD, f32), (HD, f32))
             for slot in range(2)
-        ]
-        + [pltpu.VMEM(q_base.shape, bf16), pltpu.VMEM(q_base.shape, bf16)],
+        ],
         compiler_params=PARAMS,
         name="attend",
-    )(prompt_ids, dialogue_lens, prompt_lens, arrived, q_base, kv_base, cotangent, shares)
+    )(arrived, queries, outs, stats, sloped, plain)
+    kv_grad, token = pl.pallas_call(
+        finish_kernel,
+        out_shape=(
+            jax.ShapeDtypeStruct(kv_base.shape, bf16),
+            jax.ShapeDtypeStruct((8, HD), f32),
+        ),
+        in_specs=[SMEM] + [VMEM] * 4,
+        out_specs=(VMEM, VMEM),
+        scratch_shapes=own_scratch,
+        compiler_params=PARAMS,
+        name="finish",
+    )(dialogue_lens, queries, outs, own, final)
     sums = lax.all_to_all(message, "dp", 0, 0, tiled=True)
     message = pl.pallas_call(
         steer_kernel,
         out_shape=jax.ShapeDtypeStruct((tensor, 1, steering.shape[0]), f32),
-        in_specs=[VMEM, VMEM, VMEM],
+        in_specs=[VMEM, VMEM, VMEM, VMEM],
         out_specs=VMEM,
         compiler_params=PARAMS,
         name="steer",
-    )(sums, w_query, w_kv)
+    )(sums, w_query, w_kv, token)
     parts = lax.all_to_all(message, "tensor", 0, 0, tiled=True)
     return (query_grad, kv_grad, jnp.sum(parts, axis=(0, 1)))
 

time: 98.4 us -> 97.1 us (0.987)
  blocking collectives: 59.9 us -> 39.6 us
  starting transfers between devices: 5.83 us -> 13.3 us
  Pallas kernels: 11.5 us -> 17 us
  waiting for transfers between devices: 18.3 us -> 23.6 us
    all_to_all x1 -> x0, blocking collectives: 20.3 us -> none  [shards(): sums = lax.all_to_all(message, 'dp', 0, 0, tiled=True)]
    all_to_all x0 -> x1, waiting for transfers between devices: none -> 9.59 us  [shards(): sums = lax.all_to_all(message, 'dp', 0, 0, tiled=True)]
    all_to_all x0 -> x1, starting transfers between devices: none -> 7.48 us  [shards(): sums = lax.all_to_all(message, 'dp', 0, 0, tiled=True)]
    pallas_call x0 -> x3, Pallas kernels: none -> 6.9 us  [the longest x1 3.29 us: shards(): pl.pallas_call(finish_kernel, out_shape=(jax.ShapeDtypeStruct(kv_base.sha...]
    all_to_all x1, waiting for transfers between devices: 18.3 us -> 14 us  [shards(): arrived = lax.all_to_all(outgoing, 'dp', 0, 0, tiled=True)]
    pallas_call x1, Pallas kernels: 7.83 us -> 6.44 us  [shards(): pl.pallas_call(attend_kernel, out_shape=(jax.ShapeDtypeStruct(q_base.shap...]
  transfers between devices with their start and end apart: 1 -> 2, of which waited for: 1 -> 2; matrix products, arithmetic and copies ran while one was open for 0% -> 0% of each run, Pallas kernels for 0% -> 7%
where the time goes in v4:
time: 97.1 us; the launch traced here: 96.7 us
  blocking collectives  39.6 us (41%)
  waiting for transfers between devices  23.6 us (24%)
  Pallas kernels  17 us (18%)
  starting transfers between devices  13.3 us (14%)
  between operations  2.06 us (2%)
    all_to_all x1, blocking collectives, shards(): shares = lax.all_to_all(message, 'dp', 0, 0, tiled=True)  30.8 us
    all_to_all x1, waiting for transfers between devices, shards(): arrived = lax.all_to_all(outgoing, 'dp', 0, 0, tiled=True)  14 us
    all_to_all x1, waiting for transfers between devices, shards(): sums = lax.all_to_all(message, 'dp', 0, 0, tiled=True)  9.59 us
    all_to_all x1, blocking collectives, shards(): parts = lax.all_to_all(message, 'tensor', 0, 0, tiled=True)  8.81 us
    all_to_all x1, starting transfers between devices, shards(): sums = lax.all_to_all(message, 'dp', 0, 0, tiled=True)  7.48 us
    pallas_call x1, Pallas kernels, shards(): pl.pallas_call(attend_kernel, out_shape=(jax.ShapeDtypeStruct(q_base.shap...  6.44 us
    all_to_all x1, starting transfers between devices, shards(): arrived = lax.all_to_all(outgoing, 'dp', 0, 0, tiled=True)  5.83 us
    pallas_call x1, Pallas kernels, shards(): pl.pallas_call(finish_kernel, out_shape=(jax.ShapeDtypeStruct(kv_base.sha...  3.29 us
  transfers between devices with their start and end apart: 2, of which 2 were waited for; matrix products, arithmetic and copies ran while one was open for 0% of the time, Pallas kernels for 7%

profile of v4, /device:TPU:1, one launch (start us, length us, event | category | flops | bytes accessed | tf_op | source)
XLA Modules:
  0.0 96.7 jit_solution(6696198744019456739)
XLA Ops:
  1.3 2.0 %project.1 = s16[64,2,768]{2,1,0:T(2,128)(2,1)} custom-call(s32[1]{0:T(128)S(6)} %copy.13.prompt_id.ids, f32[1,128]{1,0:T(1,128)} %bitcast.1, bf16[128,1024]{1,0:T(8,128)(2,1)} %w_query.3, bf16[2,128,128]{2,1,0:T(8,128)(2,1)} %w_kv.3), custom_call_target="tpu_custom_call" | custom-call | tf_op jit(solution)/shard_map/project/pallas_call | solution.py:328
  3.2 0.0 copy-start.3
  3.3 30.8 %all_to_all.20.shares = s16[64,2,768]{2,1,0:T(2,128)(2,1)S(1)} all-to-all(s16[64,2,768]{2,1,0:T(2,128)(2,1)} %project.1), channel_id=1, replica_groups=mesh['dp'=64,'tensor'=8] {'dp'}, dimensions={0} | all-to-all | bytes 393216 | tf_op jit(solution)/shard_map/all_to_all | solution.py:342
  34.0 0.0 copy-done.3
  34.0 0.0 copy-start.5
  34.0 1.4 %pick.1.outgoing = bf16[64,2,16,128]{3,2,1,0:T(8,128)(2,1)} custom-call(s16[64,2,768]{2,1,0:T(2,128)(2,1)S(1)} %all_to_all.20.shares, bf16[2,32,16,128]{3,2,1,0:T(8,128)(2,1)S(1)} %copy-done.3), custom_call_target="tpu_custom_call" | custom-call | tf_op jit(solution)/shard_map/pick/pallas_call | solution.py:343
  35.4 0.0 copy-start.1
  35.5 0.0 copy-start.2
  35.5 5.8 %all-to-all-start.1 = ((bf16[64,2,16,128]{3,2,1,0:T(8,128)(2,1)}), bf16[64,2,16,128]{3,2,1,0:T(8,128)(2,1)S(1)}, u32[]{:S(2)}, u32[]{:S(2)}) async-start(bf16[64,2,16,128]{3,2,1,0:T(8,128)(2,1)} %pick.1.outgoing), calls=%async_computation.1 | async-start | bytes 1048576 | tf_op jit(solution)/shard_map/all_to_all | solution.py:356
  42.0 0.0 copy-done.5
  42.0 0.0 copy-done.1
  42.0 0.0 copy-done.2
  42.0 0.5 shift.1
  42.5 0.0 copy-start.6
  42.5 0.6 copy-done.6
  43.2 3.1 %prepare.1 = (f32[256,128]{1,0:T(8,128)S(1)}, bf16[8,256,128]{2,1,0:T(8,128)(2,1)S(1)}, bf16[8,256,128]{2,1,0:T(8,128)(2,1)S(1)}) custom-call(s32[1]{0:T(128)S(6)} %copy.13.prompt_id.ids, s32[32]{0:T(128)S(1)} %copy-done.6, s32[1]{0:T(128)S(6)} %copy.14.lens, bf16[256,1024]{1,0:T(8,128)(2,1)S(1)} %get-tuple-element.14.queries, ...), custom_call_target="tpu_custom_call" | custom-call | tf_op jit(solution)/shard_map/prepare/pallas_call | solution.py:374
  46.3 14.0 %all-to-all-done.1.arrived = bf16[64,2,16,128]{3,2,1,0:T(8,128)(2,1)S(1)} async-done(((bf16[64,2,16,128]{3,2,1,0:T(8,128)(2,1)}), bf16[64,2,16,128]{3,2,1,0:T(8,128)(2,1)S(1)}, u32[]{:S(2)}, u32[]{:S(2)}) %all-to-all-start.1) | async-done | bytes 524320 | tf_op jit(solution)/shard_map/all_to_all | solution.py:356
  60.2 6.4 %attend.1 = (bf16[256,1024]{1,0:T(8,128)(2,1)}, bf16[64,2,640]{2,1,0:T(2,128)(2,1)}, f32[256,128]{1,0:T(8,128)S(1)}) custom-call(bf16[64,2,16,128]{3,2,1,0:T(8,128)(2,1)S(1)} %all-to-all-done.1.arrived, bf16[256,1024]{1,0:T(8,128)(2,1)S(1)} %get-tuple-element.14.queries, bf16[256,1024]{1,0:T(8,128)(2,1)S(1)} %get-tuple-element.15.outs, ...), custom_call_target="tpu_custom_call" | custom-call | tf_op jit(solution)/shard_map/attend/pallas_call | solution.py:383
  66.7 7.5 %all-to-all-start.2 = ((bf16[64,2,640]{2,1,0:T(2,128)(2,1)}), bf16[64,2,640]{2,1,0:T(2,128)(2,1)S(1)}, u32[]{:S(2)}, u32[]{:S(2)}) async-start(bf16[64,2,640]{2,1,0:T(2,128)(2,1)} %get-tuple-element.23), calls=%async_computation.2 | async-start | bytes 327680 | tf_op jit(solution)/shard_map/all_to_all | solution.py:417
  74.2 0.0 copy-start
  74.2 0.0 copy-start.4
  74.2 3.3 %finish.1 = (bf16[2,256,128]{2,1,0:T(8,128)(2,1)}, f32[8,128]{1,0:T(8,128)S(1)}) custom-call(s32[1]{0:T(128)S(6)} %copy.14.lens, bf16[256,1024]{1,0:T(8,128)(2,1)S(1)} %get-tuple-element.14.queries, bf16[256,1024]{1,0:T(8,128)(2,1)S(1)} %get-tuple-element.15.outs, bf16[2,256,128]{2,1,0:T(8,128)(2,1)S(1)} %get-tuple-element.16.own, ...), custom_call_target="tpu_custom_call" | custom-call | tf_op jit(solution)/shard_map/finish/pallas_call | solution.py:405
  77.5 9.6 %all-to-all-done.2.sums = bf16[64,2,640]{2,1,0:T(2,128)(2,1)S(1)} async-done(((bf16[64,2,640]{2,1,0:T(2,128)(2,1)}), bf16[64,2,640]{2,1,0:T(2,128)(2,1)S(1)}, u32[]{:S(2)}, u32[]{:S(2)}) %all-to-all-start.2) | async-done | bytes 163872 | tf_op jit(solution)/shard_map/all_to_all | solution.py:417
  87.1 0.0 copy-done
  87.1 0.0 copy-done.4
  87.1 0.3 steer.1
  87.3 8.8 %all_to_all.21 = f32[8,1,128]{2,1,0:T(1,128)S(1)} all-to-all(f32[8,1,128]{2,1,0:T(1,128)S(1)} %steer.1), channel_id=1, replica_groups=mesh['dp'=64,'tensor'=8] {'tensor'}, dimensions={0} | all-to-all | bytes 8192 | tf_op jit(solution)/shard_map/all_to_all | solution.py:426
  96.2 0.5 reduce_sum.9
Async XLA Ops:
  3.2 30.8 %copy-start.3 = (bf16[2,32,16,128]{3,2,1,0:T(8,128)(2,1)S(1)}, bf16[2,32,16,128]{3,2,1,0:T(8,128)(2,1)}, u32[]{:S(2)}) copy-start(bf16[2,32,16,128]{3,2,1,0:T(8,128)(2,1)} %cache.1) | copy-start | bytes 786436
  34.0 7.9 %copy-start.5 = (bf16[2,256,128]{2,1,0:T(8,128)(2,1)S(1)}, bf16[2,256,128]{2,1,0:T(8,128)(2,1)}, u32[]{:S(2)}) copy-start(bf16[2,256,128]{2,1,0:T(8,128)(2,1)} %kv_ref.1) | copy-start | bytes 393220
  35.4 6.5 %copy-start.1 = (bf16[256,1024]{1,0:T(8,128)(2,1)S(1)}, bf16[256,1024]{1,0:T(8,128)(2,1)}, u32[]{:S(2)}) copy-start(bf16[256,1024]{1,0:T(8,128)(2,1)} %q_ref.1) | copy-start | bytes 1572868
  35.5 6.5 %copy-start.2 = (bf16[256,1024]{1,0:T(8,128)(2,1)S(1)}, bf16[256,1024]{1,0:T(8,128)(2,1)}, u32[]{:S(2)}) copy-start(bf16[256,1024]{1,0:T(8,128)(2,1)} %cot_ref.1) | copy-start | bytes 1572868
  35.5 24.8 %all-to-all-start.1 = ((bf16[64,2,16,128]{3,2,1,0:T(8,128)(2,1)}), bf16[64,2,16,128]{3,2,1,0:T(8,128)(2,1)S(1)}, u32[]{:S(2)}, u32[]{:S(2)}) async-start(bf16[64,2,16,128]{3,2,1,0:T(8,128)(2,1)} %pick.1.outgoing), calls=%async_computation.1 | async-start | bytes 1048576 | tf_op jit(solution)/shard_map/all_to_all | solution.py:356
  42.5 0.7 copy-start.6
  66.7 20.4 %all-to-all-start.2 = ((bf16[64,2,640]{2,1,0:T(2,128)(2,1)}), bf16[64,2,640]{2,1,0:T(2,128)(2,1)S(1)}, u32[]{:S(2)}, u32[]{:S(2)}) async-start(bf16[64,2,640]{2,1,0:T(2,128)(2,1)} %get-tuple-element.23), calls=%async_computation.2 | async-start | bytes 327680 | tf_op jit(solution)/shard_map/all_to_all | solution.py:417
  74.2 12.9 %copy-start = (bf16[128,1024]{1,0:T(8,128)(2,1)S(1)}, bf16[128,1024]{1,0:T(8,128)(2,1)}, u32[]{:S(2)}) copy-start(bf16[128,1024]{1,0:T(8,128)(2,1)} %w_query.3) | copy-start | bytes 786436
  74.2 12.9 %copy-start.4 = (bf16[2,128,128]{2,1,0:T(8,128)(2,1)S(1)}, bf16[2,128,128]{2,1,0:T(8,128)(2,1)}, u32[]{:S(2)}) copy-start(bf16[2,128,128]{2,1,0:T(8,128)(2,1)} %w_kv.3) | copy-start | bytes 196612

commit v5 on v4

--- a/solution.py
+++ b/solution.py
@@ -272,8 +272,12 @@
         message[peer] = block
 
 
-def finish_kernel(lens, queries, outs, own, final, dkv_ref, token, keys_two, causal):
+def finish_kernel(
+    lens, queries, outs, own, final, dq, dq_out, dkv_ref, token, keys_two, causal, sem
+):
     bf16 = jnp.bfloat16
+    copy = pltpu.make_async_copy(dq, dq_out, sem)
+    copy.start()
     heads = queries.shape[1] // HD
     fill_own(lens[0], own[0], keys_two, causal)
     grad_keys = grad_values = None
@@ -291,6 +295,7 @@
     dkv_ref[0] = grad_keys.astype(bf16)
     dkv_ref[1] = grad_values.astype(bf16)
     token[...] = jnp.zeros_like(token)
+    copy.wait()
 
 
 def steer_kernel(sums, w_query, w_kv, token, message):
@@ -380,7 +385,7 @@
         compiler_params=PARAMS,
         name="prepare",
     )(prompt_ids, prompt_lens, dialogue_lens, queries, outs, own)
-    query_grad, message, final = pl.pallas_call(
+    held_grad, message, final = pl.pallas_call(
         attend_kernel,
         out_shape=(
             jax.ShapeDtypeStruct(q_base.shape, bf16),
@@ -402,18 +407,19 @@
         compiler_params=PARAMS,
         name="attend",
     )(arrived, queries, outs, stats, sloped, plain)
-    kv_grad, token = pl.pallas_call(
+    query_grad, kv_grad, token = pl.pallas_call(
         finish_kernel,
         out_shape=(
+            jax.ShapeDtypeStruct(q_base.shape, bf16),
             jax.ShapeDtypeStruct(kv_base.shape, bf16),
             jax.ShapeDtypeStruct((8, HD), f32),
         ),
-        in_specs=[SMEM] + [VMEM] * 4,
-        out_specs=(VMEM, VMEM),
-        scratch_shapes=own_scratch,
+        in_specs=[SMEM] + [VMEM] * 5,
+        out_specs=(HBM, VMEM, VMEM),
+        scratch_shapes=own_scratch + [pltpu.SemaphoreType.DMA],
         compiler_params=PARAMS,
         name="finish",
-    )(dialogue_lens, queries, outs, own, final)
+    )(dialogue_lens, queries, outs, own, final, held_grad)
     sums = lax.all_to_all(message, "dp", 0, 0, tiled=True)
     message = pl.pallas_call(
         steer_kernel,

time: 97.1 us -> 96.9 us (level)
  no operation moved by 1% of the time
where the time goes in v5:
time: 96.9 us; the launch traced here: 96.5 us
  blocking collectives  39.6 us (41%)
  waiting for transfers between devices  23.5 us (24%)
  Pallas kernels  16.9 us (17%)
  starting transfers between devices  13.3 us (14%)
  between operations  2.06 us (2%)
    all_to_all x1, blocking collectives, shards(): shares = lax.all_to_all(message, 'dp', 0, 0, tiled=True)  30.8 us
    all_to_all x1, waiting for transfers between devices, shards(): arrived = lax.all_to_all(outgoing, 'dp', 0, 0, tiled=True)  14 us
    all_to_all x1, waiting for transfers between devices, shards(): sums = lax.all_to_all(message, 'dp', 0, 0, tiled=True)  9.57 us
    all_to_all x1, blocking collectives, shards(): parts = lax.all_to_all(message, 'tensor', 0, 0, tiled=True)  8.8 us
    all_to_all x1, starting transfers between devices, shards(): sums = lax.all_to_all(message, 'dp', 0, 0, tiled=True)  7.49 us
    pallas_call x1, Pallas kernels, shards(): pl.pallas_call(attend_kernel, out_shape=(jax.ShapeDtypeStruct(q_base.shap...  6.29 us
    all_to_all x1, starting transfers between devices, shards(): arrived = lax.all_to_all(outgoing, 'dp', 0, 0, tiled=True)  5.83 us
    pallas_call x1, Pallas kernels, shards(): pl.pallas_call(finish_kernel, out_shape=(jax.ShapeDtypeStruct(q_base.shap...  3.3 us
  transfers between devices with their start and end apart: 2, of which 2 were waited for; matrix products, arithmetic and copies ran while one was open for 0% of the time, Pallas kernels for 7%

profile of v5, /device:TPU:1, one launch (start us, length us, event | category | flops | bytes accessed | tf_op | source)
XLA Modules:
  0.0 96.5 jit_solution(2166128963156740147)
XLA Ops:
  1.3 2.0 %project.1 = s16[64,2,768]{2,1,0:T(2,128)(2,1)} custom-call(s32[1]{0:T(128)S(6)} %copy.13.prompt_id.ids, f32[1,128]{1,0:T(1,128)} %bitcast.1, bf16[128,1024]{1,0:T(8,128)(2,1)} %w_query.3, bf16[2,128,128]{2,1,0:T(8,128)(2,1)} %w_kv.3), custom_call_target="tpu_custom_call" | custom-call | tf_op jit(solution)/shard_map/project/pallas_call | solution.py:333
  3.2 0.0 copy-start.3
  3.3 30.8 %all_to_all.20.shares = s16[64,2,768]{2,1,0:T(2,128)(2,1)S(1)} all-to-all(s16[64,2,768]{2,1,0:T(2,128)(2,1)} %project.1), channel_id=1, replica_groups=mesh['dp'=64,'tensor'=8] {'dp'}, dimensions={0} | all-to-all | bytes 393216 | tf_op jit(solution)/shard_map/all_to_all | solution.py:347
  34.0 0.0 copy-done.3
  34.0 0.0 copy-start.5
  34.0 1.4 %pick.1.outgoing = bf16[64,2,16,128]{3,2,1,0:T(8,128)(2,1)} custom-call(s16[64,2,768]{2,1,0:T(2,128)(2,1)S(1)} %all_to_all.20.shares, bf16[2,32,16,128]{3,2,1,0:T(8,128)(2,1)S(1)} %copy-done.3), custom_call_target="tpu_custom_call" | custom-call | tf_op jit(solution)/shard_map/pick/pallas_call | solution.py:348
  35.4 0.0 copy-start.1
  35.5 0.0 copy-start.2
  35.5 5.8 %all-to-all-start.1 = ((bf16[64,2,16,128]{3,2,1,0:T(8,128)(2,1)}), bf16[64,2,16,128]{3,2,1,0:T(8,128)(2,1)S(1)}, u32[]{:S(2)}, u32[]{:S(2)}) async-start(bf16[64,2,16,128]{3,2,1,0:T(8,128)(2,1)} %pick.1.outgoing), calls=%async_computation.1 | async-start | bytes 1048576 | tf_op jit(solution)/shard_map/all_to_all | solution.py:361
  42.0 0.0 copy-done.5
  42.0 0.0 copy-done.1
  42.0 0.0 copy-done.2
  42.0 0.5 shift.1
  42.5 0.0 copy-start.6
  42.5 0.6 copy-done.6
  43.2 3.1 %prepare.1 = (f32[256,128]{1,0:T(8,128)S(1)}, bf16[8,256,128]{2,1,0:T(8,128)(2,1)S(1)}, bf16[8,256,128]{2,1,0:T(8,128)(2,1)S(1)}) custom-call(s32[1]{0:T(128)S(6)} %copy.13.prompt_id.ids, s32[32]{0:T(128)S(1)} %copy-done.6, s32[1]{0:T(128)S(6)} %copy.14.lens, bf16[256,1024]{1,0:T(8,128)(2,1)S(1)} %get-tuple-element.15.queries, ...), custom_call_target="tpu_custom_call" | custom-call | tf_op jit(solution)/shard_map/prepare/pallas_call | solution.py:379
  46.3 14.0 %all-to-all-done.1.arrived = bf16[64,2,16,128]{3,2,1,0:T(8,128)(2,1)S(1)} async-done(((bf16[64,2,16,128]{3,2,1,0:T(8,128)(2,1)}), bf16[64,2,16,128]{3,2,1,0:T(8,128)(2,1)S(1)}, u32[]{:S(2)}, u32[]{:S(2)}) %all-to-all-start.1) | async-done | bytes 524320 | tf_op jit(solution)/shard_map/all_to_all | solution.py:361
  60.2 6.3 %attend.1 = (bf16[256,1024]{1,0:T(8,128)(2,1)S(1)}, bf16[64,2,640]{2,1,0:T(2,128)(2,1)}, f32[256,128]{1,0:T(8,128)S(1)}) custom-call(bf16[64,2,16,128]{3,2,1,0:T(8,128)(2,1)S(1)} %all-to-all-done.1.arrived, bf16[256,1024]{1,0:T(8,128)(2,1)S(1)} %get-tuple-element.15.queries, bf16[256,1024]{1,0:T(8,128)(2,1)S(1)} %get-tuple-element.16.outs, ...), custom_call_target="tpu_custom_call" | custom-call | tf_op jit(solution)/shard_map/attend/pallas_call | solution.py:388
  66.5 7.5 %all-to-all-start.2 = ((bf16[64,2,640]{2,1,0:T(2,128)(2,1)}), bf16[64,2,640]{2,1,0:T(2,128)(2,1)S(1)}, u32[]{:S(2)}, u32[]{:S(2)}) async-start(bf16[64,2,640]{2,1,0:T(2,128)(2,1)} %get-tuple-element.25), calls=%async_computation.2 | async-start | bytes 327680 | tf_op jit(solution)/shard_map/all_to_all | solution.py:423
  74.0 0.0 copy-start
  74.0 0.0 copy-start.4
  74.0 3.3 %finish.1 = (bf16[256,1024]{1,0:T(8,128)(2,1)}, bf16[2,256,128]{2,1,0:T(8,128)(2,1)}, f32[8,128]{1,0:T(8,128)S(1)}) custom-call(s32[1]{0:T(128)S(6)} %copy.14.lens, bf16[256,1024]{1,0:T(8,128)(2,1)S(1)} %get-tuple-element.15.queries, bf16[256,1024]{1,0:T(8,128)(2,1)S(1)} %get-tuple-element.16.outs, bf16[2,256,128]{2,1,0:T(8,128)(2,1)S(1)} %get-tuple-element.17.own, ...), custom_call_target="tpu_custom_call" | custom-call | tf_op jit(solution)/shard_map/finish/pallas_call | solution.py:410
  77.4 9.6 %all-to-all-done.2.sums = bf16[64,2,640]{2,1,0:T(2,128)(2,1)S(1)} async-done(((bf16[64,2,640]{2,1,0:T(2,128)(2,1)}), bf16[64,2,640]{2,1,0:T(2,128)(2,1)S(1)}, u32[]{:S(2)}, u32[]{:S(2)}) %all-to-all-start.2) | async-done | bytes 163872 | tf_op jit(solution)/shard_map/all_to_all | solution.py:423
  86.9 0.0 copy-done
  86.9 0.0 copy-done.4
  86.9 0.3 steer.1
  87.2 8.8 %all_to_all.21 = f32[8,1,128]{2,1,0:T(1,128)S(1)} all-to-all(f32[8,1,128]{2,1,0:T(1,128)S(1)} %steer.1), channel_id=1, replica_groups=mesh['dp'=64,'tensor'=8] {'tensor'}, dimensions={0} | all-to-all | bytes 8192 | tf_op jit(solution)/shard_map/all_to_all | solution.py:432
  96.0 0.5 reduce_sum.9
Async XLA Ops:
  3.2 30.8 %copy-start.3 = (bf16[2,32,16,128]{3,2,1,0:T(8,128)(2,1)S(1)}, bf16[2,32,16,128]{3,2,1,0:T(8,128)(2,1)}, u32[]{:S(2)}) copy-start(bf16[2,32,16,128]{3,2,1,0:T(8,128)(2,1)} %cache.1) | copy-start | bytes 786436
  34.0 7.9 %copy-start.5 = (bf16[2,256,128]{2,1,0:T(8,128)(2,1)S(1)}, bf16[2,256,128]{2,1,0:T(8,128)(2,1)}, u32[]{:S(2)}) copy-start(bf16[2,256,128]{2,1,0:T(8,128)(2,1)} %kv_ref.1) | copy-start | bytes 393220
  35.4 6.5 %copy-start.1 = (bf16[256,1024]{1,0:T(8,128)(2,1)S(1)}, bf16[256,1024]{1,0:T(8,128)(2,1)}, u32[]{:S(2)}) copy-start(bf16[256,1024]{1,0:T(8,128)(2,1)} %q_ref.1) | copy-start | bytes 1572868
  35.5 6.5 %copy-start.2 = (bf16[256,1024]{1,0:T(8,128)(2,1)S(1)}, bf16[256,1024]{1,0:T(8,128)(2,1)}, u32[]{:S(2)}) copy-start(bf16[256,1024]{1,0:T(8,128)(2,1)} %cot_ref.1) | copy-start | bytes 1572868
  35.5 24.8 %all-to-all-start.1 = ((bf16[64,2,16,128]{3,2,1,0:T(8,128)(2,1)}), bf16[64,2,16,128]{3,2,1,0:T(8,128)(2,1)S(1)}, u32[]{:S(2)}, u32[]{:S(2)}) async-start(bf16[64,2,16,128]{3,2,1,0:T(8,128)(2,1)} %pick.1.outgoing), calls=%async_computation.1 | async-start | bytes 1048576 | tf_op jit(solution)/shard_map/all_to_all | solution.py:361
  42.5 0.7 copy-start.6
  66.5 20.4 %all-to-all-start.2 = ((bf16[64,2,640]{2,1,0:T(2,128)(2,1)}), bf16[64,2,640]{2,1,0:T(2,128)(2,1)S(1)}, u32[]{:S(2)}, u32[]{:S(2)}) async-start(bf16[64,2,640]{2,1,0:T(2,128)(2,1)} %get-tuple-element.25), calls=%async_computation.2 | async-start | bytes 327680 | tf_op jit(solution)/shard_map/all_to_all | solution.py:423
  74.0 12.9 %copy-start = (bf16[128,1024]{1,0:T(8,128)(2,1)S(1)}, bf16[128,1024]{1,0:T(8,128)(2,1)}, u32[]{:S(2)}) copy-start(bf16[128,1024]{1,0:T(8,128)(2,1)} %w_query.3) | copy-start | bytes 786436
  74.0 12.9 %copy-start.4 = (bf16[2,128,128]{2,1,0:T(8,128)(2,1)S(1)}, bf16[2,128,128]{2,1,0:T(8,128)(2,1)}, u32[]{:S(2)}) copy-start(bf16[2,128,128]{2,1,0:T(8,128)(2,1)} %w_kv.3) | copy-start | bytes 196612

commit v6 on v5

--- a/solution.py
+++ b/solution.py
@@ -146,16 +146,19 @@
     heads = queries.shape[1] // HD
     fill_own(lens[0], own[0], keys_two, causal)
     prompt_live = jnp.full((queries.shape[0], 1), prompt_lens[ids[0]], jnp.int32)
-    stats[:, 3 * heads : 3 * heads + 1] = prompt_live.astype(f32)
+    stats[:, 2 * heads : 2 * heads + 1] = prompt_live.astype(f32)
     for head in range(heads):
         columns = slice(head * HD, (head + 1) * HD)
         score = dot(two_parts(queries[:, columns]), keys_two[...], NT) + causal[...]
         top = jnp.max(score, 1, keepdims=True)
         prob = jnp.exp2(score - top)
-        slope = prob * dot(outs[:, columns], own[1], NT)
-        stats[:, head : head + 1] = top
-        stats[:, heads + head : heads + head + 1] = jnp.sum(prob, 1, keepdims=True)
-        stats[:, 2 * heads + head : 2 * heads + head + 1] = jnp.sum(slope, 1, keepdims=True)
+        mass = jnp.sum(prob, 1, keepdims=True)
+        prob = prob * (1.0 / mass)
+        slope = dot(outs[:, columns], own[1], NT)
+        delta = jnp.sum(prob * slope, 1, keepdims=True)
+        slope = prob * (slope - delta)
+        stats[:, head : head + 1] = top + jnp.log2(mass)
+        stats[:, heads + head : heads + head + 1] = delta
         sloped[head] = dot(slope.astype(bf16), own[0], NN).astype(bf16)
         plain[head] = dot(prob.astype(bf16), own[0], NN).astype(bf16)
 
@@ -193,7 +196,7 @@
     keys_t[:HD] = arrived[:, 0].reshape(span, HD).T
     values_t[...] = arrived[:, 1].reshape(span, HD).T
     feature = lax.broadcasted_iota(jnp.int32, (HD, span), 0)
-    prompt_live = jnp.broadcast_to(column(stats[:8], 3 * heads), (8, HD))[:1]
+    prompt_live = jnp.broadcast_to(column(stats[:8], 2 * heads), (8, HD))[:1]
     prompt_live = jnp.concatenate([prompt_live] * (span // HD), axis=1)
     place = lax.broadcasted_iota(jnp.int32, (1, span), 1).astype(f32)
     barred = jnp.where(place >= prompt_live, MASKED, 0.0)
@@ -215,22 +218,23 @@
 
     def softmax(head, at):
         slot, rows = head % 2, slice(at * ROWS, (at + 1) * ROWS)
-        own_top, own_mass, own_slope = (column(stats[rows], n * heads + head) for n in range(3))
+        own_top, own_delta = (column(stats[rows], n * heads + head) for n in range(2))
         score = scores[slot][rows]
         top = jnp.maximum(jnp.max(score, 1, keepdims=True), own_top)
         prob = jnp.exp2(score - top)
         share = jnp.exp2(own_top - top)
         slope = slopes[slot][rows]
-        inverse = 1.0 / (jnp.sum(prob, 1, keepdims=True) + own_mass * share)
-        delta = (jnp.sum(prob * slope, 1, keepdims=True) + own_slope * share) * inverse
+        inverse = 1.0 / (jnp.sum(prob, 1, keepdims=True) + share)
+        delta = (jnp.sum(prob * slope, 1, keepdims=True) + own_delta * share) * inverse
         grads[slot][rows] = (prob * (slope - delta)).astype(bf16)
         factor = inverse * scale
         factors[slot][rows] = jnp.broadcast_to(factor, (ROWS, HD))
         own_factor = factor * share
-        term = sloped[head, rows].astype(f32) - delta * plain[head, rows].astype(f32)
+        apart = own_delta - delta
+        term = sloped[head, rows].astype(f32) + apart * plain[head, rows].astype(f32)
         terms[slot][rows] = term * own_factor
-        by_query = (own_slope - delta * own_mass) * own_factor
-        by_out = own_mass * share * inverse
+        by_query = apart * own_factor
+        by_out = share * inverse
         key_sums.append(by_query * queries[rows, columns(head)].astype(f32))
         value_sums.append(by_out * outs[rows, columns(head)].astype(f32))
         for n, value in enumerate((top, inverse, delta)):

time: 96.9 us -> 96.7 us (level)
  waiting for transfers between devices: 23.5 us -> 22 us
  Pallas kernels: 16.9 us -> 18.1 us
    all_to_all x1, waiting for transfers between devices: 14 us -> 12.4 us  [shards(): arrived = lax.all_to_all(outgoing, 'dp', 0, 0, tiled=True)]
    pallas_call x1, Pallas kernels: 3.11 us -> 4.64 us  [shards(): pl.pallas_call(prepare_kernel, out_shape=(by_row, by_head, by_head), in_s...]
  transfers between devices with their start and end apart: 2 -> 2, of which waited for: 2 -> 2; matrix products, arithmetic and copies ran while one was open for 0% -> 0% of each run, Pallas kernels for 7% -> 9%
where the time goes in v6:
time: 96.7 us; the launch traced here: 96.3 us
  blocking collectives  39.6 us (41%)
  waiting for transfers between devices  22 us (23%)
  Pallas kernels  18.1 us (19%)
  starting transfers between devices  13.3 us (14%)
  between operations  2.06 us (2%)
    all_to_all x1, blocking collectives, shards(): shares = lax.all_to_all(message, 'dp', 0, 0, tiled=True)  30.8 us
    all_to_all x1, waiting for transfers between devices, shards(): arrived = lax.all_to_all(outgoing, 'dp', 0, 0, tiled=True)  12.4 us
    all_to_all x1, waiting for transfers between devices, shards(): sums = lax.all_to_all(message, 'dp', 0, 0, tiled=True)  9.57 us
    all_to_all x1, blocking collectives, shards(): parts = lax.all_to_all(message, 'tensor', 0, 0, tiled=True)  8.81 us
    all_to_all x1, starting transfers between devices, shards(): sums = lax.all_to_all(message, 'dp', 0, 0, tiled=True)  7.47 us
    pallas_call x1, Pallas kernels, shards(): pl.pallas_call(attend_kernel, out_shape=(jax.ShapeDtypeStruct(q_base.shap...  6.02 us
    all_to_all x1, starting transfers between devices, shards(): arrived = lax.all_to_all(outgoing, 'dp', 0, 0, tiled=True)  5.83 us
    pallas_call x1, Pallas kernels, shards(): pl.pallas_call(prepare_kernel, out_shape=(by_row, by_head, by_head), in_s...  4.64 us
  transfers between devices with their start and end apart: 2, of which 2 were waited for; matrix products, arithmetic and copies ran while one was open for 0% of the time, Pallas kernels for 9%

profile of v6, /device:TPU:1, one launch (start us, length us, event | category | flops | bytes accessed | tf_op | source)
XLA Modules:
  0.0 96.3 jit_solution(6330008777280185490)
XLA Ops:
  1.3 2.0 %project.1 = s16[64,2,768]{2,1,0:T(2,128)(2,1)} custom-call(s32[1]{0:T(128)S(6)} %copy.13.prompt_id.ids, f32[1,128]{1,0:T(1,128)} %bitcast.1, bf16[128,1024]{1,0:T(8,128)(2,1)} %w_query.3, bf16[2,128,128]{2,1,0:T(8,128)(2,1)} %w_kv.3), custom_call_target="tpu_custom_call" | custom-call | tf_op jit(solution)/shard_map/project/pallas_call | solution.py:337
  3.2 0.0 copy-start.3
  3.3 30.8 %all_to_all.20.shares = s16[64,2,768]{2,1,0:T(2,128)(2,1)S(1)} all-to-all(s16[64,2,768]{2,1,0:T(2,128)(2,1)} %project.1), channel_id=1, replica_groups=mesh['dp'=64,'tensor'=8] {'dp'}, dimensions={0} | all-to-all | bytes 393216 | tf_op jit(solution)/shard_map/all_to_all | solution.py:351
  34.0 0.0 copy-done.3
  34.0 0.0 copy-start.5
  34.0 1.4 %pick.1.outgoing = bf16[64,2,16,128]{3,2,1,0:T(8,128)(2,1)} custom-call(s16[64,2,768]{2,1,0:T(2,128)(2,1)S(1)} %all_to_all.20.shares, bf16[2,32,16,128]{3,2,1,0:T(8,128)(2,1)S(1)} %copy-done.3), custom_call_target="tpu_custom_call" | custom-call | tf_op jit(solution)/shard_map/pick/pallas_call | solution.py:352
  35.4 0.0 copy-start.1
  35.5 0.0 copy-start.2
  35.5 5.8 %all-to-all-start.1 = ((bf16[64,2,16,128]{3,2,1,0:T(8,128)(2,1)}), bf16[64,2,16,128]{3,2,1,0:T(8,128)(2,1)S(1)}, u32[]{:S(2)}, u32[]{:S(2)}) async-start(bf16[64,2,16,128]{3,2,1,0:T(8,128)(2,1)} %pick.1.outgoing), calls=%async_computation.1 | async-start | bytes 1048576 | tf_op jit(solution)/shard_map/all_to_all | solution.py:365
  42.0 0.0 copy-done.5
  42.0 0.0 copy-done.1
  42.0 0.0 copy-done.2
  42.0 0.5 shift.1
  42.5 0.0 copy-start.6
  42.5 0.6 copy-done.6
  43.2 4.6 %prepare.1 = (f32[256,128]{1,0:T(8,128)S(1)}, bf16[8,256,128]{2,1,0:T(8,128)(2,1)S(1)}, bf16[8,256,128]{2,1,0:T(8,128)(2,1)S(1)}) custom-call(s32[1]{0:T(128)S(6)} %copy.13.prompt_id.ids, s32[32]{0:T(128)S(1)} %copy-done.6, s32[1]{0:T(128)S(6)} %copy.14.lens, bf16[256,1024]{1,0:T(8,128)(2,1)S(1)} %get-tuple-element.15.queries, ...), custom_call_target="tpu_custom_call" | custom-call | tf_op jit(solution)/shard_map/prepare/pallas_call | solution.py:383
  47.8 12.4 %all-to-all-done.1.arrived = bf16[64,2,16,128]{3,2,1,0:T(8,128)(2,1)S(1)} async-done(((bf16[64,2,16,128]{3,2,1,0:T(8,128)(2,1)}), bf16[64,2,16,128]{3,2,1,0:T(8,128)(2,1)S(1)}, u32[]{:S(2)}, u32[]{:S(2)}) %all-to-all-start.1) | async-done | bytes 524320 | tf_op jit(solution)/shard_map/all_to_all | solution.py:365
  60.2 6.0 %attend.1 = (bf16[256,1024]{1,0:T(8,128)(2,1)S(1)}, bf16[64,2,640]{2,1,0:T(2,128)(2,1)}, f32[256,128]{1,0:T(8,128)S(1)}) custom-call(bf16[64,2,16,128]{3,2,1,0:T(8,128)(2,1)S(1)} %all-to-all-done.1.arrived, bf16[256,1024]{1,0:T(8,128)(2,1)S(1)} %get-tuple-element.15.queries, bf16[256,1024]{1,0:T(8,128)(2,1)S(1)} %get-tuple-element.16.outs, ...), custom_call_target="tpu_custom_call" | custom-call | tf_op jit(solution)/shard_map/attend/pallas_call | solution.py:392
  66.3 7.5 %all-to-all-start.2 = ((bf16[64,2,640]{2,1,0:T(2,128)(2,1)}), bf16[64,2,640]{2,1,0:T(2,128)(2,1)S(1)}, u32[]{:S(2)}, u32[]{:S(2)}) async-start(bf16[64,2,640]{2,1,0:T(2,128)(2,1)} %get-tuple-element.25), calls=%async_computation.2 | async-start | bytes 327680 | tf_op jit(solution)/shard_map/all_to_all | solution.py:427
  73.7 0.0 copy-start
  73.8 0.0 copy-start.4
  73.8 3.3 %finish.1 = (bf16[256,1024]{1,0:T(8,128)(2,1)}, bf16[2,256,128]{2,1,0:T(8,128)(2,1)}, f32[8,128]{1,0:T(8,128)S(1)}) custom-call(s32[1]{0:T(128)S(6)} %copy.14.lens, bf16[256,1024]{1,0:T(8,128)(2,1)S(1)} %get-tuple-element.15.queries, bf16[256,1024]{1,0:T(8,128)(2,1)S(1)} %get-tuple-element.16.outs, bf16[2,256,128]{2,1,0:T(8,128)(2,1)S(1)} %get-tuple-element.17.own, ...), custom_call_target="tpu_custom_call" | custom-call | tf_op jit(solution)/shard_map/finish/pallas_call | solution.py:414
  77.1 9.6 %all-to-all-done.2.sums = bf16[64,2,640]{2,1,0:T(2,128)(2,1)S(1)} async-done(((bf16[64,2,640]{2,1,0:T(2,128)(2,1)}), bf16[64,2,640]{2,1,0:T(2,128)(2,1)S(1)}, u32[]{:S(2)}, u32[]{:S(2)}) %all-to-all-start.2) | async-done | bytes 163872 | tf_op jit(solution)/shard_map/all_to_all | solution.py:427
  86.6 0.0 copy-done
  86.7 0.0 copy-done.4
  86.7 0.3 steer.1
  86.9 8.8 %all_to_all.21 = f32[8,1,128]{2,1,0:T(1,128)S(1)} all-to-all(f32[8,1,128]{2,1,0:T(1,128)S(1)} %steer.1), channel_id=1, replica_groups=mesh['dp'=64,'tensor'=8] {'tensor'}, dimensions={0} | all-to-all | bytes 8192 | tf_op jit(solution)/shard_map/all_to_all | solution.py:436
  95.7 0.5 reduce_sum.9
Async XLA Ops:
  3.2 30.8 %copy-start.3 = (bf16[2,32,16,128]{3,2,1,0:T(8,128)(2,1)S(1)}, bf16[2,32,16,128]{3,2,1,0:T(8,128)(2,1)}, u32[]{:S(2)}) copy-start(bf16[2,32,16,128]{3,2,1,0:T(8,128)(2,1)} %cache.1) | copy-start | bytes 786436
  34.0 7.9 %copy-start.5 = (bf16[2,256,128]{2,1,0:T(8,128)(2,1)S(1)}, bf16[2,256,128]{2,1,0:T(8,128)(2,1)}, u32[]{:S(2)}) copy-start(bf16[2,256,128]{2,1,0:T(8,128)(2,1)} %kv_ref.1) | copy-start | bytes 393220
  35.4 6.5 %copy-start.1 = (bf16[256,1024]{1,0:T(8,128)(2,1)S(1)}, bf16[256,1024]{1,0:T(8,128)(2,1)}, u32[]{:S(2)}) copy-start(bf16[256,1024]{1,0:T(8,128)(2,1)} %q_ref.1) | copy-start | bytes 1572868
  35.5 6.5 %copy-start.2 = (bf16[256,1024]{1,0:T(8,128)(2,1)S(1)}, bf16[256,1024]{1,0:T(8,128)(2,1)}, u32[]{:S(2)}) copy-start(bf16[256,1024]{1,0:T(8,128)(2,1)} %cot_ref.1) | copy-start | bytes 1572868
  35.5 24.8 %all-to-all-start.1 = ((bf16[64,2,16,128]{3,2,1,0:T(8,128)(2,1)}), bf16[64,2,16,128]{3,2,1,0:T(8,128)(2,1)S(1)}, u32[]{:S(2)}, u32[]{:S(2)}) async-start(bf16[64,2,16,128]{3,2,1,0:T(8,128)(2,1)} %pick.1.outgoing), calls=%async_computation.1 | async-start | bytes 1048576 | tf_op jit(solution)/shard_map/all_to_all | solution.py:365
  42.5 0.7 copy-start.6
  66.3 20.4 %all-to-all-start.2 = ((bf16[64,2,640]{2,1,0:T(2,128)(2,1)}), bf16[64,2,640]{2,1,0:T(2,128)(2,1)S(1)}, u32[]{:S(2)}, u32[]{:S(2)}) async-start(bf16[64,2,640]{2,1,0:T(2,128)(2,1)} %get-tuple-element.25), calls=%async_computation.2 | async-start | bytes 327680 | tf_op jit(solution)/shard_map/all_to_all | solution.py:427
  73.7 12.9 %copy-start = (bf16[128,1024]{1,0:T(8,128)(2,1)S(1)}, bf16[128,1024]{1,0:T(8,128)(2,1)}, u32[]{:S(2)}) copy-start(bf16[128,1024]{1,0:T(8,128)(2,1)} %w_query.3) | copy-start | bytes 786436
  73.8 12.9 %copy-start.4 = (bf16[2,128,128]{2,1,0:T(8,128)(2,1)S(1)}, bf16[2,128,128]{2,1,0:T(8,128)(2,1)}, u32[]{:S(2)}) copy-start(bf16[2,128,128]{2,1,0:T(8,128)(2,1)} %w_kv.3) | copy-start | bytes 196612

commit v7 on v6

--- a/solution.py
+++ b/solution.py
@@ -89,15 +89,20 @@
     peers = shares.shape[0]
     last = shares.shape[2] - HD
     lane = lax.broadcasted_iota(jnp.int32, (2, HD), 1)
-    found = jnp.zeros((2, HD), jnp.int32)
-    for peer in range(peers):
-        found = jnp.where(lane == peer, shares[peer, :, last:].astype(jnp.int32), found)
-    marks[...] = found[:1]
-    copy = pltpu.make_async_copy(marks, ids, sems.at[0])
-    copy.start()
-    copy.wait()
-    for peer in range(peers):
-        pltpu.make_async_copy(cache.at[:, ids[0, peer]], outgoing.at[peer], sems.at[1]).start()
+    half = peers // 2
+    fetches = []
+    for side in range(2):
+        found = jnp.zeros((2, HD), jnp.int32)
+        for peer in range(side * half, (side + 1) * half):
+            found = jnp.where(lane == peer, shares[peer, :, last:].astype(jnp.int32), found)
+        marks[side] = found[:1]
+        fetches.append(pltpu.make_async_copy(marks.at[side], ids.at[side], sems.at[2 * side]))
+        fetches[side].start()
+    for side in range(2):
+        fetches[side].wait()
+        for peer in range(side * half, (side + 1) * half):
+            rows = cache.at[:, ids[side, 0, peer]]
+            pltpu.make_async_copy(rows, outgoing.at[peer], sems.at[1]).start()
     pltpu.make_async_copy(outgoing, outgoing, sems.at[1]).wait()
 
 
@@ -355,9 +360,9 @@
         in_specs=[VMEM, VMEM],
         out_specs=HBM,
         scratch_shapes=[
-            pltpu.VMEM((1, HD), jnp.int32),
-            pltpu.SMEM((1, HD), jnp.int32),
-            pltpu.SemaphoreType.DMA((2,)),
+            pltpu.VMEM((2, 1, HD), jnp.int32),
+            pltpu.SMEM((2, 1, HD), jnp.int32),
+            pltpu.SemaphoreType.DMA((3,)),
         ],
         compiler_params=PARAMS,
         name="pick",

time: 96.7 us -> 96.7 us (level)
  no operation moved by 1% of the time
where the time goes in v7:
time: 96.7 us; the launch traced here: 96.3 us
  blocking collectives  39.6 us (41%)
  waiting for transfers between devices  22 us (23%)
  Pallas kernels  18.1 us (19%)
  starting transfers between devices  13.3 us (14%)
  between operations  2.06 us (2%)
    all_to_all x1, blocking collectives, shards(): shares = lax.all_to_all(message, 'dp', 0, 0, tiled=True)  30.8 us
    all_to_all x1, waiting for transfers between devices, shards(): arrived = lax.all_to_all(outgoing, 'dp', 0, 0, tiled=True)  12.4 us
    all_to_all x1, waiting for transfers between devices, shards(): sums = lax.all_to_all(message, 'dp', 0, 0, tiled=True)  9.57 us
    all_to_all x1, blocking collectives, shards(): parts = lax.all_to_all(message, 'tensor', 0, 0, tiled=True)  8.81 us
    all_to_all x1, starting transfers between devices, shards(): sums = lax.all_to_all(message, 'dp', 0, 0, tiled=True)  7.47 us
    pallas_call x1, Pallas kernels, shards(): pl.pallas_call(attend_kernel, out_shape=(jax.ShapeDtypeStruct(q_base.shap...  6.02 us
    all_to_all x1, starting transfers between devices, shards(): arrived = lax.all_to_all(outgoing, 'dp', 0, 0, tiled=True)  5.83 us
    pallas_call x1, Pallas kernels, shards(): pl.pallas_call(prepare_kernel, out_shape=(by_row, by_head, by_head), in_s...  4.64 us
  transfers between devices with their start and end apart: 2, of which 2 were waited for; matrix products, arithmetic and copies ran while one was open for 0% of the time, Pallas kernels for 9%

profile of v7, /device:TPU:1, one launch (start us, length us, event | category | flops | bytes accessed | tf_op | source)
XLA Modules:
  0.0 96.3 jit_solution(3082161940615791262)
XLA Ops:
  1.3 2.0 %project.1 = s16[64,2,768]{2,1,0:T(2,128)(2,1)} custom-call(s32[1]{0:T(128)S(6)} %copy.13.prompt_id.ids, f32[1,128]{1,0:T(1,128)} %bitcast.1, bf16[128,1024]{1,0:T(8,128)(2,1)} %w_query.3, bf16[2,128,128]{2,1,0:T(8,128)(2,1)} %w_kv.3), custom_call_target="tpu_custom_call" | custom-call | tf_op jit(solution)/shard_map/project/pallas_call | solution.py:342
  3.2 0.0 copy-start.3
  3.3 30.8 %all_to_all.20.shares = s16[64,2,768]{2,1,0:T(2,128)(2,1)S(1)} all-to-all(s16[64,2,768]{2,1,0:T(2,128)(2,1)} %project.1), channel_id=1, replica_groups=mesh['dp'=64,'tensor'=8] {'dp'}, dimensions={0} | all-to-all | bytes 393216 | tf_op jit(solution)/shard_map/all_to_all | solution.py:356
  34.0 0.0 copy-done.3
  34.0 0.0 copy-start.5
  34.0 1.4 %pick.1.outgoing = bf16[64,2,16,128]{3,2,1,0:T(8,128)(2,1)} custom-call(s16[64,2,768]{2,1,0:T(2,128)(2,1)S(1)} %all_to_all.20.shares, bf16[2,32,16,128]{3,2,1,0:T(8,128)(2,1)S(1)} %copy-done.3), custom_call_target="tpu_custom_call" | custom-call | tf_op jit(solution)/shard_map/pick/pallas_call | solution.py:357
  35.4 0.0 copy-start.1
  35.5 0.0 copy-start.2
  35.5 5.8 %all-to-all-start.1 = ((bf16[64,2,16,128]{3,2,1,0:T(8,128)(2,1)}), bf16[64,2,16,128]{3,2,1,0:T(8,128)(2,1)S(1)}, u32[]{:S(2)}, u32[]{:S(2)}) async-start(bf16[64,2,16,128]{3,2,1,0:T(8,128)(2,1)} %pick.1.outgoing), calls=%async_computation.1 | async-start | bytes 1048576 | tf_op jit(solution)/shard_map/all_to_all | solution.py:370
  41.9 0.0 copy-done.5
  42.0 0.0 copy-done.1
  42.0 0.0 copy-done.2
  42.0 0.5 shift.1
  42.5 0.0 copy-start.6
  42.5 0.6 copy-done.6
  43.1 4.6 %prepare.1 = (f32[256,128]{1,0:T(8,128)S(1)}, bf16[8,256,128]{2,1,0:T(8,128)(2,1)S(1)}, bf16[8,256,128]{2,1,0:T(8,128)(2,1)S(1)}) custom-call(s32[1]{0:T(128)S(6)} %copy.13.prompt_id.ids, s32[32]{0:T(128)S(1)} %copy-done.6, s32[1]{0:T(128)S(6)} %copy.14.lens, bf16[256,1024]{1,0:T(8,128)(2,1)S(1)} %get-tuple-element.15.queries, ...), custom_call_target="tpu_custom_call" | custom-call | tf_op jit(solution)/shard_map/prepare/pallas_call | solution.py:388
  47.8 12.4 %all-to-all-done.1.arrived = bf16[64,2,16,128]{3,2,1,0:T(8,128)(2,1)S(1)} async-done(((bf16[64,2,16,128]{3,2,1,0:T(8,128)(2,1)}), bf16[64,2,16,128]{3,2,1,0:T(8,128)(2,1)S(1)}, u32[]{:S(2)}, u32[]{:S(2)}) %all-to-all-start.1) | async-done | bytes 524320 | tf_op jit(solution)/shard_map/all_to_all | solution.py:370
  60.2 6.0 %attend.1 = (bf16[256,1024]{1,0:T(8,128)(2,1)S(1)}, bf16[64,2,640]{2,1,0:T(2,128)(2,1)}, f32[256,128]{1,0:T(8,128)S(1)}) custom-call(bf16[64,2,16,128]{3,2,1,0:T(8,128)(2,1)S(1)} %all-to-all-done.1.arrived, bf16[256,1024]{1,0:T(8,128)(2,1)S(1)} %get-tuple-element.15.queries, bf16[256,1024]{1,0:T(8,128)(2,1)S(1)} %get-tuple-element.16.outs, ...), custom_call_target="tpu_custom_call" | custom-call | tf_op jit(solution)/shard_map/attend/pallas_call | solution.py:397
  66.3 7.5 %all-to-all-start.2 = ((bf16[64,2,640]{2,1,0:T(2,128)(2,1)}), bf16[64,2,640]{2,1,0:T(2,128)(2,1)S(1)}, u32[]{:S(2)}, u32[]{:S(2)}) async-start(bf16[64,2,640]{2,1,0:T(2,128)(2,1)} %get-tuple-element.25), calls=%async_computation.2 | async-start | bytes 327680 | tf_op jit(solution)/shard_map/all_to_all | solution.py:432
  73.7 0.0 copy-start
  73.7 0.0 copy-start.4
  73.8 3.3 %finish.1 = (bf16[256,1024]{1,0:T(8,128)(2,1)}, bf16[2,256,128]{2,1,0:T(8,128)(2,1)}, f32[8,128]{1,0:T(8,128)S(1)}) custom-call(s32[1]{0:T(128)S(6)} %copy.14.lens, bf16[256,1024]{1,0:T(8,128)(2,1)S(1)} %get-tuple-element.15.queries, bf16[256,1024]{1,0:T(8,128)(2,1)S(1)} %get-tuple-element.16.outs, bf16[2,256,128]{2,1,0:T(8,128)(2,1)S(1)} %get-tuple-element.17.own, ...), custom_call_target="tpu_custom_call" | custom-call | tf_op jit(solution)/shard_map/finish/pallas_call | solution.py:419
  77.1 9.6 %all-to-all-done.2.sums = bf16[64,2,640]{2,1,0:T(2,128)(2,1)S(1)} async-done(((bf16[64,2,640]{2,1,0:T(2,128)(2,1)}), bf16[64,2,640]{2,1,0:T(2,128)(2,1)S(1)}, u32[]{:S(2)}, u32[]{:S(2)}) %all-to-all-start.2) | async-done | bytes 163872 | tf_op jit(solution)/shard_map/all_to_all | solution.py:432
  86.6 0.0 copy-done
  86.6 0.0 copy-done.4
  86.6 0.3 steer.1
  86.9 8.8 %all_to_all.21 = f32[8,1,128]{2,1,0:T(1,128)S(1)} all-to-all(f32[8,1,128]{2,1,0:T(1,128)S(1)} %steer.1), channel_id=1, replica_groups=mesh['dp'=64,'tensor'=8] {'tensor'}, dimensions={0} | all-to-all | bytes 8192 | tf_op jit(solution)/shard_map/all_to_all | solution.py:441
  95.7 0.5 reduce_sum.9
Async XLA Ops:
  3.2 30.8 %copy-start.3 = (bf16[2,32,16,128]{3,2,1,0:T(8,128)(2,1)S(1)}, bf16[2,32,16,128]{3,2,1,0:T(8,128)(2,1)}, u32[]{:S(2)}) copy-start(bf16[2,32,16,128]{3,2,1,0:T(8,128)(2,1)} %cache.1) | copy-start | bytes 786436
  34.0 7.9 %copy-start.5 = (bf16[2,256,128]{2,1,0:T(8,128)(2,1)S(1)}, bf16[2,256,128]{2,1,0:T(8,128)(2,1)}, u32[]{:S(2)}) copy-start(bf16[2,256,128]{2,1,0:T(8,128)(2,1)} %kv_ref.1) | copy-start | bytes 393220
  35.4 6.5 %copy-start.1 = (bf16[256,1024]{1,0:T(8,128)(2,1)S(1)}, bf16[256,1024]{1,0:T(8,128)(2,1)}, u32[]{:S(2)}) copy-start(bf16[256,1024]{1,0:T(8,128)(2,1)} %q_ref.1) | copy-start | bytes 1572868
  35.5 6.5 %copy-start.2 = (bf16[256,1024]{1,0:T(8,128)(2,1)S(1)}, bf16[256,1024]{1,0:T(8,128)(2,1)}, u32[]{:S(2)}) copy-start(bf16[256,1024]{1,0:T(8,128)(2,1)} %cot_ref.1) | copy-start | bytes 1572868
  35.5 24.8 %all-to-all-start.1 = ((bf16[64,2,16,128]{3,2,1,0:T(8,128)(2,1)}), bf16[64,2,16,128]{3,2,1,0:T(8,128)(2,1)S(1)}, u32[]{:S(2)}, u32[]{:S(2)}) async-start(bf16[64,2,16,128]{3,2,1,0:T(8,128)(2,1)} %pick.1.outgoing), calls=%async_computation.1 | async-start | bytes 1048576 | tf_op jit(solution)/shard_map/all_to_all | solution.py:370
  42.5 0.7 copy-start.6
  66.3 20.4 %all-to-all-start.2 = ((bf16[64,2,640]{2,1,0:T(2,128)(2,1)}), bf16[64,2,640]{2,1,0:T(2,128)(2,1)S(1)}, u32[]{:S(2)}, u32[]{:S(2)}) async-start(bf16[64,2,640]{2,1,0:T(2,128)(2,1)} %get-tuple-element.25), calls=%async_computation.2 | async-start | bytes 327680 | tf_op jit(solution)/shard_map/all_to_all | solution.py:432
  73.7 12.9 %copy-start = (bf16[128,1024]{1,0:T(8,128)(2,1)S(1)}, bf16[128,1024]{1,0:T(8,128)(2,1)}, u32[]{:S(2)}) copy-start(bf16[128,1024]{1,0:T(8,128)(2,1)} %w_query.3) | copy-start | bytes 786436
  73.7 12.9 %copy-start.4 = (bf16[2,128,128]{2,1,0:T(8,128)(2,1)S(1)}, bf16[2,128,128]{2,1,0:T(8,128)(2,1)}, u32[]{:S(2)}) copy-start(bf16[2,128,128]{2,1,0:T(8,128)(2,1)} %w_kv.3) | copy-start | bytes 196612
